TPU v7x, 512 devices: a whole 4x4x16 slice. The times are simulated.
512 devices in a mesh: ctx: 64 (over x, z_hi, y), tp: 8 (over z_lo, core).
Axes of the slice: x: 4, y: 4, z: 16 (z_hi: 4, z_lo: 4; z = z_hi * 4 + z_lo), core: 2. Of those that a mesh axis runs over, the one named last changes fastest.
Arguments:
- query_self: bfloat16 [8192, 8192], P('ctx', 'tp'), may hold values from -256 to 256
- key_value_self: bfloat16 [2, 8192, 1024], P(None, 'ctx', 'tp'), may hold values from -10 to 10
- query_cross: bfloat16 [8192, 8192], P('ctx', 'tp'), may hold values from -256 to 256
- panels: bfloat16 [2, 64, 64, 1024], P(None, 'ctx', 'tp'), may hold values from -10 to 10
- image_span: int32 [64, 2], replicated, may hold values from 0 to 8192, as said below
- panel_image: int32 [64], replicated, may hold values from 0 to 63, as said below
- cross_gate: float32 [1], replicated, may hold values from 0.5 to 2
Outputs:
- self_out: bfloat16 [8192, 8192], P('ctx', 'tp')
- cross_out: bfloat16 [8192, 8192], P('ctx', 'tp')
Inputs may be any that keep to these rules, and one draw needn't show every extreme that they name: `image_span`: images come in groups of one to four consecutive images that share one range; the ranges of groups are disjoint, in order, and together cover all 8192 tokens; every image whose number is a multiple of 4 starts a group; image i (i > 0) opens its own range or lies in a group whose range begins at or before i * 128, and any range that begins with image i begins strictly inside tokens i * 128 to (i + 1) * 128 - 1, except image 0 at token 0; the last range ends at 8192. `panel_image`: each image is stored in exactly one slot, and slot p holds an image of the same aligned block of 4 slots (p // 4 equal).
All inputs are finite; a program needn't handle non-finite values.
Results may differ from a plain program's by a relative error of at most 0.0045.
Values may be sent and summed in bfloat16 or wider, within the bound.
A program may use at most 64 MiB of HBM per device.

v0:
```python
import jax
import jax.numpy as jnp
from jax import lax
from jax.sharding import PartitionSpec as P

HEAD_SIZE = 128


NEG_FILL = -1e30


def shifted(array, axis, by):
    count = lax.axis_size(axis)
    pairs = [(i, i + by) for i in range(count) if 0 <= i + by < count]
    return lax.ppermute(array, axis, pairs)


def softmax_update(current, queries, key_row_block, value_rows, allowed):
    maximum, totals, summed = current
    scaling = queries.shape[3] ** (-0.5)
    scores = (
        jnp.einsum("tkgd,nkd->kgtn", queries, key_row_block, preferred_element_type=jnp.float32)
        * scaling
    )
    visible = allowed[None, None]
    scores = jnp.where(visible, scores, NEG_FILL)
    updated = jnp.maximum(maximum, jnp.max(scores, axis=3))
    factor = jnp.exp(maximum - updated)
    weights = jnp.where(visible, jnp.exp(scores - updated[..., None]), 0.0)
    totals = totals * factor + jnp.sum(weights, axis=3)
    summed = summed * factor[..., None] + jnp.einsum(
        "kgtn,nkd->kgtd",
        weights.astype(jnp.bfloat16),
        value_rows,
        preferred_element_type=jnp.float32,
    )
    return (updated, totals, summed)


def finish(current, row_count, columns):
    maximum, totals, summed = current
    result = summed / totals[..., None]
    return result.transpose(2, 0, 1, 3).reshape(row_count, columns)


def pick_stride():
    for candidate in (8, 5, 4, 3, 2):
        return candidate
    return 1


def local(query_self, key_value_self, query_cross, panels, image_span, panel_image, cross_gate):
    row_count, columns = query_self.shape
    head_dim = HEAD_SIZE
    kv_heads = key_value_self.shape[2] // head_dim
    group_size = columns // head_dim // kv_heads
    image_total = panel_image.shape[0]
    own_index = lax.axis_index("ctx")
    first_row = own_index * row_count
    positions = first_row + jnp.arange(row_count, dtype=jnp.int32)
    caption_queries = query_self.reshape(row_count, kv_heads, group_size, head_dim)
    vision_queries = query_cross.reshape(row_count, kv_heads, group_size, head_dim)
    initial = (
        jnp.full((kv_heads, group_size, row_count), NEG_FILL, jnp.float32),
        jnp.zeros((kv_heads, group_size, row_count), jnp.float32),
        jnp.zeros((kv_heads, group_size, row_count, head_dim), jnp.float32),
    )
    panel_heads = lax.all_to_all(panels, "tp", split_axis=3, concat_axis=2, tiled=True)
    own_slots = panel_heads.shape[1]
    every_text = lax.all_gather(key_value_self, "ctx", axis=1, tiled=True)
    length = every_text.shape[1]
    stride = 512

    def text_advance(block_index, running):
        offset = 0 + block_index * stride
        block_rows = lax.dynamic_slice_in_dim(every_text, block_index * stride, stride, 1)
        key_row_block = block_rows[0].reshape(stride, kv_heads, head_dim)
        value_rows = block_rows[1].reshape(stride, kv_heads, head_dim)
        allowed = (offset + jnp.arange(stride, dtype=jnp.int32))[None, :] <= positions[:, None]
        return softmax_update(running, caption_queries, key_row_block, value_rows, allowed)

    text_state = lax.fori_loop(0, length // stride, text_advance, initial)
    nearby = []
    for distance in range(4, -4, -1):
        if distance == 0:
            nearby.append(panel_heads)
        else:
            nearby.append(shifted(panel_heads, "ctx", distance))
    segment = jnp.concatenate(nearby, axis=1)
    raw_slots = (own_index - 4) * own_slots + jnp.arange(8 * own_slots, dtype=jnp.int32)
    valid = (raw_slots >= 0) & (raw_slots < image_total)
    slot_ids = jnp.where(valid, raw_slots, -1)
    length = segment.shape[1]
    image_rows = segment.shape[2]
    image_stride = pick_stride()
    slot_range = jnp.arange(image_total, dtype=jnp.int32)

    def image_advance(block_index, running):
        slot_match = slot_ids[:, None] == slot_range[None, :]
        image_ids = jnp.sum(jnp.where(slot_match, panel_image[None, :] + 1, 0), axis=1) - 1
        matches = image_ids[:, None] == slot_range[None, :]
        opening = jnp.sum(jnp.where(matches, image_span[None, :, 0], 0), axis=1)
        closing = jnp.sum(jnp.where(matches, image_span[None, :, 1], 0), axis=1)
        reading = (positions[:, None] >= opening[None, :]) & (positions[:, None] < closing[None, :])
        allowed = jnp.repeat(reading, image_rows, axis=1)
        key_row_block = segment[0].reshape(image_stride * image_rows, kv_heads, head_dim)
        value_rows = segment[1].reshape(image_stride * image_rows, kv_heads, head_dim)
        return softmax_update(running, vision_queries, key_row_block, value_rows, allowed)

    image_state = lax.fori_loop(0, length // image_stride, image_advance, initial)
    self_out = finish(text_state, row_count, columns).astype(jnp.bfloat16)
    cross_out = (jnp.tanh(cross_gate[0]) * finish(image_state, row_count, columns)).astype(
        jnp.bfloat16
    )
    return (self_out, cross_out)


def solution(mesh):
    return jax.shard_map(
        local,
        mesh=mesh,
        in_specs=(
            P("ctx", "tp"),
            P(None, "ctx", "tp"),
            P("ctx", "tp"),
            P(None, "ctx", "tp", None),
            P(),
            P(),
            P(),
        ),
        out_specs=(P("ctx", "tp"), P("ctx", "tp")),
        check_vma=False,
    )
```

profile of v0, /device:TPU:6, one launch (start us, length us, event | category | flops | bytes accessed | tf_op | source)
XLA Modules:
  0.0 228.8 jit_solution(8584340182394832259)
XLA Ops:
  7.9 1.1 copy.69
  9.0 1.1 reshape.198
  10.1 5.9 %all-to-all-start = ((bf16[8,2,1024]{2,1,0:T(2,128)(2,1)}), bf16[8,2,1024]{2,1,0:T(2,128)(2,1)S(1)}, u32[]{:S(2)}, u32[]{:S(2)}) async-start(bf16[8,2,1024]{2,1,0:T(2,128)(2,1)} %reshape.198), calls=%async_computation | async-start | bytes 65536 | tf_op jit(solution)/shard_map/all_to_all | solution.py:68
  17.8 3.9 %all-to-all-done = bf16[8,2,1024]{2,1,0:T(2,128)(2,1)S(1)} async-done(((bf16[8,2,1024]{2,1,0:T(2,128)(2,1)}), bf16[8,2,1024]{2,1,0:T(2,128)(2,1)S(1)}, u32[]{:S(2)}, u32[]{:S(2)}) %all-to-all-start) | async-done | bytes 32800 | tf_op jit(solution)/shard_map/all_to_all | solution.py:68
  22.7 9.1 %collective-permute-start = (bf16[2,1,64,128]{3,2,0,1:T(8,128)(2,1)S(1)}, bf16[2,1,64,128]{3,2,0,1:T(8,128)(2,1)S(1)}, u32[]{:S(2)}, u32[]{:S(2)}) collective-permute-start(bf16[2,1,64,128]{3,2,0,1:T(8,128)(2,1)S(1)} %bitcast.144), channel_id=1, source_target_pairs={{0,32},{8,40},{16,48},{24,56},{32,64},{40,72},{48,80},{56,88},{64,... | collective-permute-start | bytes 98312 | tf_op jit(solution)/shard_map/ppermute | solution.py:15
  33.0 4.9 %collective-permute-start.1 = (bf16[2,1,64,128]{3,2,0,1:T(8,128)(2,1)S(1)}, bf16[2,1,64,128]{3,2,0,1:T(8,128)(2,1)S(1)}, u32[]{:S(2)}, u32[]{:S(2)}) collective-permute-start(bf16[2,1,64,128]{3,2,0,1:T(8,128)(2,1)S(1)} %bitcast.145), channel_id=1, source_target_pairs={{0,24},{8,32},{16,40},{24,48},{32,56},{40,64},{48,72},{56,80},{64,... | collective-permute-start | bytes 98312 | tf_op jit(solution)/shard_map/ppermute | solution.py:15
  37.9 6.5 %collective-permute-start.2 = (bf16[2,1,64,128]{3,2,0,1:T(8,128)(2,1)S(1)}, bf16[2,1,64,128]{3,2,0,1:T(8,128)(2,1)S(1)}, u32[]{:S(2)}, u32[]{:S(2)}) collective-permute-start(bf16[2,1,64,128]{3,2,0,1:T(8,128)(2,1)S(1)} %bitcast.146), channel_id=1, source_target_pairs={{0,16},{8,24},{16,32},{24,40},{32,48},{40,56},{48,64},{56,72},{64,... | collective-permute-start | bytes 98312 | tf_op jit(solution)/shard_map/ppermute | solution.py:15
  44.5 2.9 %collective-permute-start.3 = (bf16[2,1,64,128]{3,2,0,1:T(8,128)(2,1)S(1)}, bf16[2,1,64,128]{3,2,0,1:T(8,128)(2,1)S(1)}, u32[]{:S(2)}, u32[]{:S(2)}) collective-permute-start(bf16[2,1,64,128]{3,2,0,1:T(8,128)(2,1)S(1)} %bitcast.147), channel_id=1, source_target_pairs={{0,8},{8,16},{16,24},{24,32},{32,40},{40,48},{48,56},{56,64},{64,7... | collective-permute-start | bytes 98312 | tf_op jit(solution)/shard_map/ppermute | solution.py:15
  47.4 9.9 %collective-permute-start.4 = (bf16[2,1,64,128]{3,2,0,1:T(8,128)(2,1)S(1)}, bf16[2,1,64,128]{3,2,0,1:T(8,128)(2,1)S(1)}, u32[]{:S(2)}, u32[]{:S(2)}) collective-permute-start(bf16[2,1,64,128]{3,2,0,1:T(8,128)(2,1)S(1)} %bitcast.148), channel_id=1, source_target_pairs={{8,0},{16,8},{24,16},{32,24},{40,32},{48,40},{56,48},{64,56},{72,6... | collective-permute-start | bytes 98312 | tf_op jit(solution)/shard_map/ppermute | solution.py:15
  57.3 1.9 collective-permute-start.5
  59.2 3.6 %collective-permute-start.6 = (bf16[2,1,64,128]{3,2,0,1:T(8,128)(2,1)S(1)}, bf16[2,1,64,128]{3,2,0,1:T(8,128)(2,1)S(1)}, u32[]{:S(2)}, u32[]{:S(2)}) collective-permute-start(bf16[2,1,64,128]{3,2,0,1:T(8,128)(2,1)S(1)} %bitcast.150), channel_id=1, source_target_pairs={{24,0},{32,8},{40,16},{48,24},{56,32},{64,40},{72,48},{80,56},{88,... | collective-permute-start | bytes 98312 | tf_op jit(solution)/shard_map/ppermute | solution.py:15
  62.9 1.7 collective-permute-done.5
  64.6 1.6 collective-permute-done.6
  68.0 0.9 copy.75
  68.8 89.6 %all-gather.2.cloned.1.call-done = bf16[2,8192,128]{2,1,0:T(8,128)(2,1)} async-done(((bf16[2,128,128]{2,1,0:T(8,128)(2,1)}), bf16[2,8192,128]{2,1,0:T(8,128)(2,1)}) %all-gather.2.cloned.1.call-update) | async-done | bytes 4194320 | tf_op jit(solution)/shard_map/all_gather | solution.py:70
  158.4 62.4 %while.5 = (s32[]{:T(128)}, f32[1,8,128]{2,1,0:T(8,128)S(1)}, f32[1,8,128]{2,1,0:T(8,128)S(1)}, f32[1,8,128,128]{3,2,1,0:T(8,128)S(1)}, bf16[2,8192,128]{2,1,0:T...) while((s32[]{:T(128)}, f32[1,8,128]{2,1,0:T(8,128)S(1)}, ...), condition=%wide.region_3.4_spmd.clone, body=%wide.region_0.3_spmd.clone.sunk | while | flops 275716736 | bytes 8197335 | solution.py:82
  158.6 1.4 fusion.52
  160.5 1.8 fusion.55
  162.5 1.4 fusion.52
  164.4 1.8 fusion.55
  166.4 1.4 fusion.52
  168.3 1.8 fusion.55
  170.3 1.4 fusion.52
  172.2 1.8 fusion.55
  174.2 1.4 fusion.52
  176.1 1.8 fusion.55
  178.1 1.4 fusion.52
  180.0 1.8 fusion.55
  182.0 1.4 fusion.52
  183.9 1.8 fusion.55
  185.8 1.4 fusion.52
  187.8 1.8 fusion.55
  189.7 1.4 fusion.52
  191.7 1.8 fusion.55
  193.6 1.4 fusion.52
  195.6 1.8 fusion.55
  197.5 1.4 fusion.52
  199.5 1.8 fusion.55
  201.4 1.4 fusion.52
  203.4 1.8 fusion.55
  205.3 1.4 fusion.52
  207.3 1.8 fusion.55
  209.2 1.4 fusion.52
  211.2 1.8 fusion.55
  213.1 1.4 fusion.52
  215.1 1.8 fusion.55
  217.0 1.4 fusion.52
  219.0 1.8 fusion.55
  (156 shorter events, 17.6 us)
Async XLA Ops:
  7.2 59.1 %copy-start = (bf16[128,1024]{1,0:T(8,128)(2,1)S(1)}, bf16[128,1024]{1,0:T(8,128)(2,1)}, u32[]{:S(2)}) copy-start(bf16[128,1024]{1,0:T(8,128)(2,1)} %param.11) | copy-start | bytes 786436
  7.2 24.8 %copy-start.1 = (bf16[128,1024]{1,0:T(8,128)(2,1)S(1)}, bf16[128,1024]{1,0:T(8,128)(2,1)}, u32[]{:S(2)}) copy-start(bf16[128,1024]{1,0:T(8,128)(2,1)} %param.9) | copy-start | bytes 786436
  7.2 151.2 %all-gather.2.cloned.1.call-start = ((), (), s32[]{:S(2)}) async-start(), calls=%async_computation.1 | async-start | bytes 4259840 | tf_op jit(solution)/shard_map/all_gather | solution.py:70
  10.1 11.6 %all-to-all-start = ((bf16[8,2,1024]{2,1,0:T(2,128)(2,1)}), bf16[8,2,1024]{2,1,0:T(2,128)(2,1)S(1)}, u32[]{:S(2)}, u32[]{:S(2)}) async-start(bf16[8,2,1024]{2,1,0:T(2,128)(2,1)} %reshape.198), calls=%async_computation | async-start | bytes 65536 | tf_op jit(solution)/shard_map/all_to_all | solution.py:68
  22.7 34.5 %collective-permute-start = (bf16[2,1,64,128]{3,2,0,1:T(8,128)(2,1)S(1)}, bf16[2,1,64,128]{3,2,0,1:T(8,128)(2,1)S(1)}, u32[]{:S(2)}, u32[]{:S(2)}) collective-permute-start(bf16[2,1,64,128]{3,2,0,1:T(8,128)(2,1)S(1)} %bitcast.144), channel_id=1, source_target_pairs={{0,32},{8,40},{16,48},{24,56},{32,64},{40,72},{48,80},{56,88},{64,... | collective-permute-start | bytes 98312 | tf_op jit(solution)/shard_map/ppermute | solution.py:15
  33.0 26.2 %collective-permute-start.1 = (bf16[2,1,64,128]{3,2,0,1:T(8,128)(2,1)S(1)}, bf16[2,1,64,128]{3,2,0,1:T(8,128)(2,1)S(1)}, u32[]{:S(2)}, u32[]{:S(2)}) collective-permute-start(bf16[2,1,64,128]{3,2,0,1:T(8,128)(2,1)S(1)} %bitcast.145), channel_id=1, source_target_pairs={{0,24},{8,32},{16,40},{24,48},{32,56},{40,64},{48,72},{56,80},{64,... | collective-permute-start | bytes 98312 | tf_op jit(solution)/shard_map/ppermute | solution.py:15
  37.9 24.9 %collective-permute-start.2 = (bf16[2,1,64,128]{3,2,0,1:T(8,128)(2,1)S(1)}, bf16[2,1,64,128]{3,2,0,1:T(8,128)(2,1)S(1)}, u32[]{:S(2)}, u32[]{:S(2)}) collective-permute-start(bf16[2,1,64,128]{3,2,0,1:T(8,128)(2,1)S(1)} %bitcast.146), channel_id=1, source_target_pairs={{0,16},{8,24},{16,32},{24,40},{32,48},{40,56},{48,64},{56,72},{64,... | collective-permute-start | bytes 98312 | tf_op jit(solution)/shard_map/ppermute | solution.py:15
  44.5 18.4 %collective-permute-start.3 = (bf16[2,1,64,128]{3,2,0,1:T(8,128)(2,1)S(1)}, bf16[2,1,64,128]{3,2,0,1:T(8,128)(2,1)S(1)}, u32[]{:S(2)}, u32[]{:S(2)}) collective-permute-start(bf16[2,1,64,128]{3,2,0,1:T(8,128)(2,1)S(1)} %bitcast.147), channel_id=1, source_target_pairs={{0,8},{8,16},{16,24},{24,32},{32,40},{40,48},{48,56},{56,64},{64,7... | collective-permute-start | bytes 98312 | tf_op jit(solution)/shard_map/ppermute | solution.py:15
  47.4 15.5 %collective-permute-start.4 = (bf16[2,1,64,128]{3,2,0,1:T(8,128)(2,1)S(1)}, bf16[2,1,64,128]{3,2,0,1:T(8,128)(2,1)S(1)}, u32[]{:S(2)}, u32[]{:S(2)}) collective-permute-start(bf16[2,1,64,128]{3,2,0,1:T(8,128)(2,1)S(1)} %bitcast.148), channel_id=1, source_target_pairs={{8,0},{16,8},{24,16},{32,24},{40,32},{48,40},{56,48},{64,56},{72,6... | collective-permute-start | bytes 98312 | tf_op jit(solution)/shard_map/ppermute | solution.py:15
  57.3 7.3 %collective-permute-start.5 = (bf16[2,1,64,128]{3,2,0,1:T(8,128)(2,1)S(1)}, bf16[2,1,64,128]{3,2,0,1:T(8,128)(2,1)S(1)}, u32[]{:S(2)}, u32[]{:S(2)}) collective-permute-start(bf16[2,1,64,128]{3,2,0,1:T(8,128)(2,1)S(1)} %bitcast.149), channel_id=1, source_target_pairs={{16,0},{24,8},{32,16},{40,24},{48,32},{56,40},{64,48},{72,56},{80,... | collective-permute-start | bytes 98312 | tf_op jit(solution)/shard_map/ppermute | solution.py:15
  59.2 7.0 %collective-permute-start.6 = (bf16[2,1,64,128]{3,2,0,1:T(8,128)(2,1)S(1)}, bf16[2,1,64,128]{3,2,0,1:T(8,128)(2,1)S(1)}, u32[]{:S(2)}, u32[]{:S(2)}) collective-permute-start(bf16[2,1,64,128]{3,2,0,1:T(8,128)(2,1)S(1)} %bitcast.150), channel_id=1, source_target_pairs={{24,0},{32,8},{40,16},{48,24},{56,32},{64,40},{72,48},{80,56},{88,... | collective-permute-start | bytes 98312 | tf_op jit(solution)/shard_map/ppermute | solution.py:15
Sparse Core Ops, SparseCore 0:
  12.2 146.1 all-gather.1
where the time goes:
time: 230 us; the launch traced here: 229 us
  waiting for transfers between devices  97.5 us (42%)
  matrix products  51.1 us (22%)
  starting transfers between devices  44.7 us (19%)
  between operations  15 us (7%)
  other arithmetic  12.6 us (5%)
  local copies, waits for them, and re-layouts  6.23 us (3%)
    all_gather x1, waiting for transfers between devices, local(): every_text = lax.all_gather(key_value_self, 'ctx', axis=1, tiled=True)  89.6 us
    ppermute x7, starting transfers between devices, shifted(): return lax.ppermute(array, axis, pairs)  38.8 us
    dot_general x17, matrix products, softmax_update(): jnp.einsum('kgtn,nkd->kgtd', weights.astype(jnp.bfloat16), value_rows, pr...  28.8 us
    dot_general x17, matrix products, softmax_update(): jnp.einsum('tkgd,nkd->kgtn', queries, key_row_block, preferred_element_ty...  22.3 us
    reduce_sum x17, other arithmetic, softmax_update(): totals = totals * factor + jnp.sum(weights, axis=3)  8.71 us
    all_to_all x1, starting transfers between devices, local(): lax.all_to_all(panels, 'tp', split_axis=3, concat_axis=2, tiled=True)  5.9 us
    unnamed x18, local copies, waits for them, and re-layouts  4.87 us
  transfers between devices with their start and end apart: 9, of which 4 were waited for; matrix products, arithmetic and copies ran while one was open for 3% of the time, Pallas kernels for 0%

commit v1 on v0

v1 whole, which is shorter than its diff:
```python
import math

import jax
import jax.numpy as jnp
from jax import lax
from jax.experimental import pallas as pl
from jax.experimental.pallas import tpu as pltpu
from jax.sharding import PartitionSpec as P

MESH = pl.DeviceIdType.MESH
F32 = jnp.float32
BF16 = jnp.bfloat16
HEAD = 128
GROUP = 8
TOK = 128
COLS = GROUP * TOK
ROW = 4 * TOK
START = -1e30
HIDDEN = -1e38
EXPONENT = HEAD**-0.5 * math.log2(math.e)
NT = (((1,), (1,)), ((), ()))
ORIGIN = (0, 3, 1, 2)


def kernel(
    span, slot_image, gate, q_self, kv_own, q_cross, panels, self_out, cross_out,
    qs, kv, staged, pan, acc, top, tot, part_out, part_in, stat_out, stat_in,
    z_send, z_recv, x_send, x_recv, y_send, y_recv, r_send, r_recv,
    q_send, q_recv, o_send, o_recv, p_send, p_recv, s_send, s_recv,
):
    ctx = lax.axis_index("ctx")
    tp = lax.axis_index("tp")
    x, z, y = ctx // 16, (ctx // 4) % 4, ctx % 4
    bundle = ctx // 4

    def at(xx, zz, yy):
        return xx * 16 + zz * 4 + yy

    def origin(zi):
        if isinstance(zi, int):
            return (z + ORIGIN[zi]) % 4
        return (z + jnp.where(zi == 0, 0, jnp.where(zi == 1, 3, zi - 1))) % 4

    def remote(src, dst, send, recv, where):
        return pltpu.make_async_remote_copy(
            src_ref=src, dst_ref=dst, send_sem=send, recv_sem=recv, device_id=where, device_id_type=MESH
        )

    barrier = pltpu.get_barrier_semaphore()
    for d in (1, 2, 3):
        for peer in (at((x + d) % 4, z, y), at(x, (z + d) % 4, y), at(x, z, (y + d) % 4)):
            pl.semaphore_signal(barrier, inc=1, device_id=(peer, tp), device_id_type=MESH)
    for d in range(1, 8):
        pl.semaphore_signal(barrier, inc=1, device_id=(ctx, (tp + d) % 8), device_id_type=MESH)

    @pl.when((y == 0) & (bundle > 0))
    def _():
        for d in range(4):
            pl.semaphore_signal(barrier, inc=1, device_id=(ctx - 4 + d, tp), device_id_type=MESH)

    kv[0, ctx] = kv_own[0]
    kv[1, ctx] = kv_own[1]
    for h in range(GROUP):
        qs[0, pl.ds(h * TOK, TOK)] = q_self[:, h * HEAD : (h + 1) * HEAD]
    pair = jnp.concatenate([panels[0, 0].astype(F32), panels[1, 0].astype(F32)], axis=0)
    for h in range(GROUP):
        staged[h] = pair[:, h * HEAD : (h + 1) * HEAD].astype(BF16)

    pl.semaphore_wait(barrier, jnp.where(bundle < 15, 17, 16))

    def z_copy(kind, d):
        target = (z + {1: 1, 2: 3, 3: 2}[d]) % 4
        block = kv.at[kind, ctx]
        return remote(block, block, z_send.at[d, kind], z_recv.at[d, kind], (at(x, target, y), tp))

    def z_wait(kind, zi):
        block = kv.at[kind, at(x, origin(zi), y)]
        remote(block, block, z_send.at[0, 0], z_recv.at[zi, kind], (ctx, (tp + 1) % 8)).wait_recv()

    def item(i):
        if i < 2:
            return i, x
        if i == 2:
            return 0, x - 1
        return jnp.where(x == 3, 0, 1), jnp.where(x == 3, 1, x - 1)

    def y_copy(zi, i, way, yy):
        kind, plane = item(i)
        to = {0: (y + 1) % 4, 1: (y + 3) % 4, 2: (y + 2) % 4}[way]
        block = kv.at[kind, at(plane, origin(zi), yy)]
        return remote(block, block, y_send.at[zi, i, way], y_recv.at[zi, i, way], (at(x, z, to), tp))

    def y_onward(zi, i):
        kind, plane = item(i)
        up = i != 2
        from_y = (y + 3) % 4 if up else (y + 1) % 4
        to = (y + 1) % 4 if up else (y + 3) % 4
        block = kv.at[kind, at(plane, origin(zi), from_y)]
        return remote(block, block, y_send.at[zi, i, 2], y_recv.at[zi, i, 2], (at(x, z, to), tp))

    def y_wait(zi, i, way):
        kind, plane = item(i)
        yy = {0: (y + 3) % 4, 1: (y + 1) % 4, 2: (y + 2) % 4}[way]
        block = kv.at[kind, at(plane, origin(zi), yy)]
        remote(block, block, z_send.at[0, 0], y_recv.at[zi, i, way], (ctx, (tp + 1) % 8)).wait_recv()

    def x_copy(zi, kind, i, plane):
        block = kv.at[kind, at(x, origin(zi), y)]
        lane = 2 if plane is not None else kind
        to = x + 1 if plane is None else plane
        return remote(block, block, x_send.at[zi, lane], x_recv.at[zi, i], (at(to, z, y), tp))

    def x_wait(zi, i):
        kind, plane = item(i)
        block = kv.at[kind, at(plane, origin(zi), y)]
        remote(block, block, z_send.at[0, 0], x_recv.at[zi, i], (ctx, (tp + 1) % 8)).wait_recv()

    def row_copy(zi, plane, to, slot):
        rows = kv.at[1, pl.ds(at(plane, origin(zi), 0), 4)]
        return remote(rows, rows, r_send.at[zi], r_recv.at[zi, slot], (at(to, z, y), tp))

    def row_wait(zi, plane, slot):
        rows = kv.at[1, pl.ds(at(plane, origin(zi), 0), 4)]
        remote(rows, rows, z_send.at[0, 0], r_recv.at[zi, slot], (ctx, (tp + 1) % 8)).wait_recv()

    def q_copy():
        return remote(qs.at[0], qs.at[x - 1], q_send, q_recv.at[x - 1], (at(0, z, y), tp))

    def q_wait(slot):
        remote(qs.at[slot], qs.at[slot], q_send, q_recv.at[slot], (ctx, (tp + 1) % 8)).wait_recv()

    def o_copies(slot):
        to = (at(slot + 1, z, y), tp)
        return (
            remote(part_out.at[slot - 1], part_in, o_send.at[slot - 1, 0], o_recv.at[0], to),
            remote(stat_out.at[slot - 1], stat_in, o_send.at[slot - 1, 1], o_recv.at[1], to),
        )

    def p_copy(d):
        to = (tp + d) % 8
        return remote(staged.at[to], pan.at[y, tp], p_send.at[d], p_recv.at[d], (ctx, to))

    def p_wait(d):
        block = pan.at[y, (tp + 8 - d) % 8]
        remote(block, block, p_send.at[0], p_recv.at[d], (ctx, (tp + 1) % 8)).wait_recv()

    def s_copy(d):
        return remote(pan.at[y], pan.at[y], s_send.at[d], s_recv.at[d], (at(x, z, (y + d) % 4), tp))

    def s_wait(d):
        block = pan.at[(y + 4 - d) % 4]
        remote(block, block, s_send.at[d], s_recv.at[d], (ctx, (tp + 1) % 8)).wait_recv()

    def next_copy():
        return remote(pan.at[y], pan.at[4 + y], s_send.at[0], s_recv.at[4 + y], (ctx - y + 4, tp))

    def next_wait(d):
        block = pan.at[4 + d]
        remote(block, block, s_send.at[0], s_recv.at[4 + d], (ctx, (tp + 1) % 8)).wait_recv()

    def part1(zi):
        if not isinstance(zi, int) or zi > 0:
            z_wait(0, zi)

        @pl.when(x < 3)
        def _():
            x_copy(zi, 0, 2, None).start()

        @pl.when(x == 1)
        def _():
            x_copy(zi, 0, 3, 3).start()

        y_copy(zi, 0, 0, y).start()
        y_copy(zi, 0, 1, y).start()
        if not isinstance(zi, int) or zi > 0:
            z_wait(1, zi)

        @pl.when(x < 2)
        def _():
            x_copy(zi, 1, 3, None).start()

        for way in range(3):
            y_copy(zi, 1, way, y).start()

    def part2(zi):
        @pl.when(x > 0)
        def _():
            for i in (2, 3):
                x_wait(zi, i)
                y_copy(zi, i, 0, y).start()
                y_copy(zi, i, 1, y).start()

        y_wait(zi, 0, 0)
        y_onward(zi, 0).start()
        y_wait(zi, 0, 1)

    def part3(zi):
        for way in range(3):
            y_wait(zi, 1, way)

        @pl.when(x == 1)
        def _():
            row_copy(zi, 1, 0, 0).start()

        @pl.when(x == 2)
        def _():
            row_copy(zi, 2, 3, 0).start()

        @pl.when(x > 0)
        def _():
            for i in (2, 3):
                y_wait(zi, i, 0)
                if i == 3:
                    y_onward(zi, i).start()
                y_wait(zi, i, 1)
                if i == 2:
                    y_onward(zi, i).start()

    def part4(zi):
        @pl.when(x == 0)
        def _():
            row_wait(zi, 1, 0)
            row_copy(zi, 1, 3, 1).start()

    def reset(slot):
        acc[slot] = jnp.zeros((HEAD, COLS), F32)
        top[slot] = jnp.full((8, COLS), START, F32)
        tot[slot] = jnp.zeros((8, COLS), F32)

    def attend(slot, keys, values, hide):
        s = lax.dot_general(keys, qs[slot], NT, preferred_element_type=F32)
        s = hide(s)
        before = top[slot]
        now = jnp.maximum(before, jnp.max(s, axis=0, keepdims=True))
        p = jnp.exp2((s - now[:1]) * EXPONENT)
        scale = jnp.exp2((before - now) * EXPONENT)
        top[slot] = now
        tot[slot] = tot[slot] * scale + jnp.sum(p.reshape(-1, 8, COLS), axis=0)
        acc[slot] = acc[slot] * scale[:1] + jnp.dot(
            values.T, p.astype(BF16), preferred_element_type=F32
        )

    def row(kind, plane, zz):
        return kv[kind, pl.ds(at(plane, zz, 0), 4)].reshape(ROW, HEAD)

    token = lax.broadcasted_iota(jnp.int32, (1, COLS), 1) % TOK

    def attend_row(slot, plane, zz, causal):
        def hide(s):
            if not causal:
                return s
            key = at(plane, zz, 0) * TOK + lax.broadcasted_iota(jnp.int32, (ROW, COLS), 0)
            return jnp.where(key <= ctx * TOK + token, s, HIDDEN)

        attend(slot, row(0, plane, zz), row(1, plane, zz), hide)

    def attend_panels():
        reset(3)
        for h in range(GROUP):
            qs[3, pl.ds(h * TOK, TOK)] = q_cross[:, h * HEAD : (h + 1) * HEAD]
        for d in (1, 2, 3):
            s_wait(d)
        before = (y == 0) & (bundle > 0)

        @pl.when(before)
        def _():
            for d in range(4):
                next_wait(d)

        def half(which, _):
            block = pan[pl.ds(which * 4, 4)].reshape(32, 16, HEAD).astype(F32)
            keys = block[:, :8].reshape(256, HEAD).astype(BF16)
            values = block[:, 8:].reshape(256, HEAD).astype(BF16)
            here = ctx * TOK + token
            masks = []
            for k in range(4):
                image = slot_image[(bundle - which) * 4 + k]
                reads = (here >= span[image * 2]) & (here < span[image * 2 + 1])
                masks.append(jnp.broadcast_to(jnp.where(reads, 0.0, HIDDEN), (64, COLS)))
            mask = jnp.concatenate(masks, axis=0)
            attend(3, keys, values, lambda s: s + mask)
            return 0

        lax.fori_loop(0, jnp.where(before, 2, 1), half, 0)
        factor = jnp.tanh(jnp.full((1, COLS), gate[0], F32)) / jnp.sum(tot[3], axis=0, keepdims=True)
        for h in range(GROUP):
            c = slice(h * TOK, (h + 1) * TOK)
            cross_out[:, h * HEAD : (h + 1) * HEAD] = (acc[3, :, c] * factor[:, c]).T.astype(BF16)

    for kind in range(2):
        z_copy(kind, 1).start()
        z_copy(kind, 2).start()
    part1(0)
    for d in range(1, 8):
        p_copy(d).start()
    for kind in range(2):
        z_copy(kind, 3).start()

    @pl.when(x >= 2)
    def _():
        q_copy().start()

    pan[y, tp] = staged[tp]
    reset(0)

    @pl.when(x == 0)
    def _():
        reset(1)
        reset(2)

    part2(0)
    for d in range(1, 8):
        p_wait(d)
    for d in (1, 2, 3):
        s_copy(d).start()

    @pl.when(bundle < 15)
    def _():
        next_copy().start()

    part3(0)
    part1(1)

    def turn(zi, _):
        zz = origin(zi)

        @pl.when(zi < 3)
        def _():
            part2(zi + 1)

        y_wait(zi, 0, 2)

        @pl.when(zz <= z)
        def _():
            attend_row(0, x, zz, True)

        @pl.when(zi < 2)
        def _():
            part1(zi + 2)

        part4(zi)

        @pl.when(zi < 3)
        def _():
            part3(zi + 1)

        @pl.when(x > 0)
        def _():
            y_wait(zi, 2, 2)
            y_wait(zi, 3, 2)

        @pl.when(x == 3)
        def _():
            row_wait(zi, 2, 0)

        @pl.when((x == 0) & (zi == 0))
        def _():
            q_wait(1)
            q_wait(2)

        attend_row(jnp.where(x == 0, 1, 0), jnp.where(x == 0, 0, x - 1), zz, False)

        @pl.when(x == 3)
        def _():
            row_wait(zi, 1, 1)

        @pl.when((x == 0) | (x == 3))
        def _():
            attend_row(jnp.where(x == 0, 2, 0), jnp.where(x == 0, 0, 1), zz, False)

        @pl.when(zi == 0)
        def _():
            attend_panels()

        return 0

    lax.fori_loop(0, 4, turn, 0)

    @pl.when(x == 0)
    def _():
        upper = lax.broadcasted_iota(jnp.int32, (8, COLS), 0) < 4
        for slot in (1, 2):
            total = jnp.sum(tot[slot], axis=0, keepdims=True)
            part_out[slot - 1] = (acc[slot] * (1.0 / total)).astype(BF16)
            stat_out[slot - 1] = jnp.where(upper, top[slot], total)
            for copy in o_copies(slot):
                copy.start()

    @pl.when(x >= 2)
    def _():
        for copy in o_copies(1):
            copy.wait_recv()
        other_top, other_tot = stat_in[0:1], stat_in[4:5]
        own_top = top[0, 0:1]
        both = jnp.maximum(own_top, other_top)
        own = jnp.exp2((own_top - both) * EXPONENT)
        other = other_tot * jnp.exp2((other_top - both) * EXPONENT)
        acc[0] = acc[0] * own + part_in[...].astype(F32) * other
        first = lax.broadcasted_iota(jnp.int32, (8, COLS), 0) == 0
        tot[0] = tot[0] * own + jnp.where(first, other, 0.0)

    inverse = 1.0 / jnp.sum(tot[0], axis=0, keepdims=True)
    for h in range(GROUP):
        c = slice(h * TOK, (h + 1) * TOK)
        self_out[:, h * HEAD : (h + 1) * HEAD] = (acc[0, :, c] * inverse[:, c]).T.astype(BF16)

    for d in (1, 2, 3):
        for kind in range(2):
            z_copy(kind, d).wait_send()
        s_copy(d).wait_send()
    for d in range(1, 8):
        p_copy(d).wait_send()

    @pl.when(bundle < 15)
    def _():
        next_copy().wait_send()

    def drain(zi, _):
        for i in (0, 1):
            for way in range(3):
                y_copy(zi, i, way, y).wait_send()

        @pl.when(x > 0)
        def _():
            for i in (2, 3):
                for way in range(3):
                    y_copy(zi, i, way, y).wait_send()

        @pl.when(x < 3)
        def _():
            x_copy(zi, 0, 2, None).wait_send()
            row_copy(zi, 1, 3, 1).wait_send()

        @pl.when(x < 2)
        def _():
            x_copy(zi, 1, 3, None).wait_send()

        @pl.when(x == 1)
        def _():
            x_copy(zi, 0, 3, 3).wait_send()

        return 0

    lax.fori_loop(0, 4, drain, 0)

    @pl.when(x >= 2)
    def _():
        q_copy().wait_send()

    @pl.when(x == 0)
    def _():
        for slot in (1, 2):
            for copy in o_copies(slot):
                copy.wait_send()


def local(query_self, key_value_self, query_cross, panels, image_span, panel_image, cross_gate):
    smem = pl.BlockSpec(memory_space=pltpu.SMEM)
    vmem = pl.BlockSpec(memory_space=pltpu.VMEM)
    dma = pltpu.SemaphoreType.DMA
    shape = jax.ShapeDtypeStruct((TOK, COLS), BF16)
    return pl.pallas_call(
        kernel,
        out_shape=(shape, shape),
        in_specs=[smem] * 3 + [vmem] * 4,
        out_specs=(vmem, vmem),
        scratch_shapes=[
            pltpu.VMEM((4, COLS, HEAD), BF16),
            pltpu.VMEM((2, 64, TOK, HEAD), BF16),
            pltpu.VMEM((8, 16, HEAD), BF16),
            pltpu.VMEM((8, 8, 16, HEAD), BF16),
            pltpu.VMEM((4, HEAD, COLS), F32),
            pltpu.VMEM((4, 8, COLS), F32),
            pltpu.VMEM((4, 8, COLS), F32),
            pltpu.VMEM((2, HEAD, COLS), BF16),
            pltpu.VMEM((HEAD, COLS), BF16),
            pltpu.VMEM((2, 8, COLS), F32),
            pltpu.VMEM((8, COLS), F32),
            dma((4, 2)), dma((4, 2)),
            dma((4, 3)), dma((4, 4)),
            dma((4, 4, 3)), dma((4, 4, 3)),
            dma((4,)), dma((4, 2)),
            dma, dma((3,)),
            dma((2, 2)), dma((2,)),
            dma((8,)), dma((8,)),
            dma((4,)), dma((8,)),
        ],
        compiler_params=pltpu.CompilerParams(
            collective_id=0, has_side_effects=True, vmem_limit_bytes=48 << 20
        ),
        name="attention",
    )(image_span.reshape(-1), panel_image, cross_gate, query_self, key_value_self, query_cross, panels)


def solution(mesh):
    return jax.shard_map(
        local,
        mesh=mesh,
        in_specs=(
            P("ctx", "tp"),
            P(None, "ctx", "tp"),
            P("ctx", "tp"),
            P(None, "ctx", "tp", None),
            P(),
            P(),
            P(),
        ),
        out_specs=(P("ctx", "tp"), P("ctx", "tp")),
        check_vma=False,
    )
```

time: 230 us -> 66.6 us (0.29)
  the two profiles are of different devices: /device:TPU:6 before, /device:TPU:70 now
where the time goes in v1:
time: 66.6 us; the launch traced here: 66.3 us
  Pallas kernels  60.1 us (90%)
  local copies, waits for them, and re-layouts  4.82 us (7%)
  between operations  1.36 us (2%)
    pallas_call x1, Pallas kernels, local(): pl.pallas_call(kernel, out_shape=(shape, shape), in_specs=[smem] * 3 + [v...  60.1 us
    unnamed x15, local copies, waits for them, and re-layouts  4.68 us

profile of v1, /device:TPU:70, one launch (start us, length us, event | category | flops | bytes accessed | tf_op | source)
XLA Modules:
  0.0 66.3 jit_solution(17677587355190036652)
XLA Ops:
  0.6 0.0 copy-start.5
  0.6 0.0 copy-start.2
  1.3 0.0 copy-done.5
  1.3 0.1 copy.10
  1.4 0.0 copy-start.4
  1.4 0.1 reshape.7.span
  1.6 0.0 copy-done.2
  1.6 0.5 copy-done.4
  2.1 0.0 copy-start
  2.1 0.9 %copy-done = bf16[128,1024]{1,0:T(8,128)(2,1)S(1)} copy-done((bf16[128,1024]{1,0:T(8,128)(2,1)S(1)}, bf16[128,1024]{1,0:T(8,128)(2,1)}, u32[]{:S(2)}) %copy-start) | copy-done | bytes 262168
  3.0 0.0 copy-start.1
  3.1 0.9 %copy-done.1 = bf16[128,1024]{1,0:T(8,128)(2,1)S(1)} copy-done((bf16[128,1024]{1,0:T(8,128)(2,1)S(1)}, bf16[128,1024]{1,0:T(8,128)(2,1)}, u32[]{:S(2)}) %copy-start.1) | copy-done | bytes 262168
  4.0 0.0 copy-start.3
  4.0 0.8 %copy-done.3 = bf16[2,1,8,1024]{3,2,1,0:T(8,128)(2,1)S(1)} copy-done((bf16[2,1,8,1024]{3,2,1,0:T(8,128)(2,1)S(1)}, bf16[2,1,8,1024]{3,2,1,0:T(8,128)(2,1)}, u32[]{:S(2)}) %copy-start.3) | copy-done | bytes 32792
  4.8 60.1 %attention.1 = (bf16[128,1024]{1,0:T(8,128)(2,1)S(1)}, bf16[128,1024]{1,0:T(8,128)(2,1)S(1)}) custom-call(s32[128]{0:T(128)S(1)} %reshape.7.span, s32[64]{0:T(128)S(1)} %copy-done.4, f32[1]{0:T(128)S(6)} %copy.13.gate, bf16[128,1024]{1,0:T(8,128)(2,1)S(1)} %copy-done, bf16[2,128,128]{2,1,0:T(8,128)(2,1)S(1)} %copy-done.2, bf16[128,1024]{1,0:T(8,128)(2,1)S(1)} %copy-done.1, ...), custom_call_target="tpu_custom_call" | custom-call | tf_op jit(solution)/shard_map/attention/pallas_call | solution.py:462
  64.9 0.7 %copy.14 = bf16[128,1024]{1,0:T(8,128)(2,1)} copy(bf16[128,1024]{1,0:T(8,128)(2,1)S(1)} %get-tuple-element.4) | data formatting | bytes 524288
  65.6 0.7 %copy.15 = bf16[128,1024]{1,0:T(8,128)(2,1)} copy(bf16[128,1024]{1,0:T(8,128)(2,1)S(1)} %get-tuple-element.5) | data formatting | bytes 524288
Async XLA Ops:
  0.6 0.7 %copy-start.5 = (s32[64,2]{0,1:T(2,128)S(1)}, s32[64,2]{0,1:T(2,128)}, u32[]{:S(2)}) copy-start(s32[64,2]{0,1:T(2,128)} %param.11) | copy-start | bytes 1540
  0.6 0.9 %copy-start.2 = (bf16[2,128,128]{2,1,0:T(8,128)(2,1)S(1)}, bf16[2,128,128]{2,1,0:T(8,128)(2,1)}, u32[]{:S(2)}) copy-start(bf16[2,128,128]{2,1,0:T(8,128)(2,1)} %kv_own.1) | copy-start | bytes 196612
  1.4 0.7 %copy-start.4 = (s32[64]{0:T(128)S(1)}, s32[64]{0:T(128)}, u32[]{:S(2)}) copy-start(s32[64]{0:T(128)} %slot_image.1) | copy-start | bytes 772
  2.1 0.9 %copy-start = (bf16[128,1024]{1,0:T(8,128)(2,1)S(1)}, bf16[128,1024]{1,0:T(8,128)(2,1)}, u32[]{:S(2)}) copy-start(bf16[128,1024]{1,0:T(8,128)(2,1)} %q_self.1) | copy-start | bytes 786436
  3.0 0.9 %copy-start.1 = (bf16[128,1024]{1,0:T(8,128)(2,1)S(1)}, bf16[128,1024]{1,0:T(8,128)(2,1)}, u32[]{:S(2)}) copy-start(bf16[128,1024]{1,0:T(8,128)(2,1)} %q_cross.1) | copy-start | bytes 786436
  4.0 0.8 %copy-start.3 = (bf16[2,1,8,1024]{3,2,1,0:T(8,128)(2,1)S(1)}, bf16[2,1,8,1024]{3,2,1,0:T(8,128)(2,1)}, u32[]{:S(2)}) copy-start(bf16[2,1,8,1024]{3,2,1,0:T(8,128)(2,1)} %panels.1) | copy-start | bytes 98308

commit v2 on v1

--- a/solution.py
+++ b/solution.py
@@ -26,7 +26,7 @@
     span, slot_image, gate, q_self, kv_own, q_cross, panels, self_out, cross_out,
     qs, kv, staged, pan, acc, top, tot, part_out, part_in, stat_out, stat_in,
     z_send, z_recv, x_send, x_recv, y_send, y_recv, r_send, r_recv,
-    q_send, q_recv, o_send, o_recv, p_send, p_recv, s_send, s_recv,
+    q_send, q_recv, o_send, o_recv, p_send, p_recv, s_send, s_recv, panel_in, in_sem,
 ):
     ctx = lax.axis_index("ctx")
     tp = lax.axis_index("tp")
@@ -45,6 +45,11 @@
         return pltpu.make_async_remote_copy(
             src_ref=src, dst_ref=dst, send_sem=send, recv_sem=recv, device_id=where, device_id_type=MESH
         )
+
+    def reset(slot):
+        acc[slot] = jnp.zeros((HEAD, COLS), F32)
+        top[slot] = jnp.full((8, COLS), START, F32)
+        tot[slot] = jnp.zeros((8, COLS), F32)
 
     barrier = pltpu.get_barrier_semaphore()
     for d in (1, 2, 3):
@@ -58,24 +63,62 @@
         for d in range(4):
             pl.semaphore_signal(barrier, inc=1, device_id=(ctx - 4 + d, tp), device_id_type=MESH)
 
-    kv[0, ctx] = kv_own[0]
-    kv[1, ctx] = kv_own[1]
-    for h in range(GROUP):
-        qs[0, pl.ds(h * TOK, TOK)] = q_self[:, h * HEAD : (h + 1) * HEAD]
-    pair = jnp.concatenate([panels[0, 0].astype(F32), panels[1, 0].astype(F32)], axis=0)
+    own_kv = [pltpu.make_async_copy(kv_own.at[k], kv.at[k, ctx], in_sem.at[k]) for k in range(2)]
+    own_panel = pltpu.make_async_copy(panels, panel_in, in_sem.at[2])
+
+    def load_queries(array, slot, sem):
+        return [
+            pltpu.make_async_copy(
+                array.at[:, pl.ds(h * HEAD, HEAD)], qs.at[slot, pl.ds(h * TOK, TOK)], in_sem.at[sem]
+            )
+            for h in range(GROUP)
+        ]
+
+    for copy in own_kv + [own_panel] + load_queries(q_self, 0, 3) + load_queries(q_cross, 3, 4):
+        copy.start()
+
+    def wait_queries(slot, sem):
+        pltpu.make_async_copy(qs.at[slot], qs.at[slot], in_sem.at[sem]).wait()
+
+    reset(0)
+
+    @pl.when(x == 0)
+    def _():
+        reset(1)
+        reset(2)
+
+    own_panel.wait()
+    pair = jnp.concatenate([panel_in[0, 0].astype(F32), panel_in[1, 0].astype(F32)], axis=0)
     for h in range(GROUP):
         staged[h] = pair[:, h * HEAD : (h + 1) * HEAD].astype(BF16)
 
+    for copy in own_kv:
+        copy.wait()
     pl.semaphore_wait(barrier, jnp.where(bundle < 15, 17, 16))
 
     def z_copy(kind, d):
-        target = (z + {1: 1, 2: 3, 3: 2}[d]) % 4
+        target = (z + {1: 1, 2: 3}[d]) % 4
         block = kv.at[kind, ctx]
         return remote(block, block, z_send.at[d, kind], z_recv.at[d, kind], (at(x, target, y), tp))
 
+    def z_half(kind, zz, half):
+        return kv.at[kind, at(x, zz, y), pl.ds(half * 64, 64)]
+
+    def z_onward(kind, half):
+        step = 3 if half == 0 else 1
+        block = z_half(kind, (z + step) % 4, half)
+        where = (at(x, (z + 4 - step) % 4, y), tp)
+        return remote(block, block, z_send.at[3 * half, kind], z_recv.at[3 * half, kind], where)
+
     def z_wait(kind, zi):
-        block = kv.at[kind, at(x, origin(zi), y)]
-        remote(block, block, z_send.at[0, 0], z_recv.at[zi, kind], (ctx, (tp + 1) % 8)).wait_recv()
+        aside = (ctx, (tp + 1) % 8)
+        if zi < 3:
+            block = kv.at[kind, at(x, origin(zi), y)]
+            remote(block, block, z_send.at[0, 0], z_recv.at[zi, kind], aside).wait_recv()
+            return
+        for half in range(2):
+            block = z_half(kind, origin(3), half)
+            remote(block, block, z_send.at[0, 0], z_recv.at[3 * half, kind], aside).wait_recv()
 
     def item(i):
         if i < 2:
@@ -106,7 +149,7 @@
 
     def x_copy(zi, kind, i, plane):
         block = kv.at[kind, at(x, origin(zi), y)]
-        lane = 2 if plane is not None else kind
+        lane = kind if plane is None else 2
         to = x + 1 if plane is None else plane
         return remote(block, block, x_send.at[zi, lane], x_recv.at[zi, i], (at(to, z, y), tp))
 
@@ -115,9 +158,9 @@
         block = kv.at[kind, at(plane, origin(zi), y)]
         remote(block, block, z_send.at[0, 0], x_recv.at[zi, i], (ctx, (tp + 1) % 8)).wait_recv()
 
-    def row_copy(zi, plane, to, slot):
-        rows = kv.at[1, pl.ds(at(plane, origin(zi), 0), 4)]
-        return remote(rows, rows, r_send.at[zi], r_recv.at[zi, slot], (at(to, z, y), tp))
+    def row_copy(zi):
+        rows = kv.at[1, pl.ds(at(x, origin(zi), 0), 4)]
+        return remote(rows, rows, r_send.at[zi], r_recv.at[zi, 2 - x], (at(3, z, y), tp))
 
     def row_wait(zi, plane, slot):
         rows = kv.at[1, pl.ds(at(plane, origin(zi), 0), 4)]
@@ -158,9 +201,11 @@
         block = pan.at[4 + d]
         remote(block, block, s_send.at[0], s_recv.at[4 + d], (ctx, (tp + 1) % 8)).wait_recv()
 
-    def part1(zi):
-        if not isinstance(zi, int) or zi > 0:
+    def keys_out(zi):
+        if zi > 0:
             z_wait(0, zi)
+        if zi in (1, 2):
+            z_onward(0, zi - 1).start()
 
         @pl.when(x < 3)
         def _():
@@ -172,8 +217,12 @@
 
         y_copy(zi, 0, 0, y).start()
         y_copy(zi, 0, 1, y).start()
-        if not isinstance(zi, int) or zi > 0:
+
+    def values_out(zi):
+        if zi > 0:
             z_wait(1, zi)
+        if zi in (1, 2):
+            z_onward(1, zi - 1).start()
 
         @pl.when(x < 2)
         def _():
@@ -182,50 +231,45 @@
         for way in range(3):
             y_copy(zi, 1, way, y).start()
 
-    def part2(zi):
+    def spread(zi, i):
         @pl.when(x > 0)
         def _():
-            for i in (2, 3):
-                x_wait(zi, i)
-                y_copy(zi, i, 0, y).start()
-                y_copy(zi, i, 1, y).start()
-
+            x_wait(zi, i)
+            y_copy(zi, i, 0, y).start()
+            y_copy(zi, i, 1, y).start()
+
+    def rows_out(zi):
+        for way in range(3):
+            y_wait(zi, 1, way)
+
+        @pl.when((x == 1) | (x == 2))
+        def _():
+            row_copy(zi).start()
+
+    def own_onward(zi):
         y_wait(zi, 0, 0)
         y_onward(zi, 0).start()
         y_wait(zi, 0, 1)
 
-    def part3(zi):
-        for way in range(3):
-            y_wait(zi, 1, way)
-
-        @pl.when(x == 1)
-        def _():
-            row_copy(zi, 1, 0, 0).start()
-
-        @pl.when(x == 2)
-        def _():
-            row_copy(zi, 2, 3, 0).start()
-
+    def onward(zi):
         @pl.when(x > 0)
         def _():
-            for i in (2, 3):
-                y_wait(zi, i, 0)
-                if i == 3:
-                    y_onward(zi, i).start()
-                y_wait(zi, i, 1)
-                if i == 2:
-                    y_onward(zi, i).start()
-
-    def part4(zi):
-        @pl.when(x == 0)
-        def _():
-            row_wait(zi, 1, 0)
-            row_copy(zi, 1, 3, 1).start()
-
-    def reset(slot):
-        acc[slot] = jnp.zeros((HEAD, COLS), F32)
-        top[slot] = jnp.full((8, COLS), START, F32)
-        tot[slot] = jnp.zeros((8, COLS), F32)
+            y_wait(zi, 2, 1)
+            y_onward(zi, 2).start()
+            y_wait(zi, 2, 0)
+            y_wait(zi, 3, 0)
+            y_onward(zi, 3).start()
+            y_wait(zi, 3, 1)
+
+    def panels_out():
+        for d in range(1, 8):
+            p_wait(d)
+        for d in (1, 2, 3):
+            s_copy(d).start()
+
+        @pl.when(bundle < 15)
+        def _():
+            next_copy().start()
 
     def attend(slot, keys, values, hide):
         s = lax.dot_general(keys, qs[slot], NT, preferred_element_type=F32)
@@ -245,19 +289,18 @@
 
     token = lax.broadcasted_iota(jnp.int32, (1, COLS), 1) % TOK
 
-    def attend_row(slot, plane, zz, causal):
+    def attend_row(slot, plane, zz):
+        offset = jnp.where(slot > 0, TOK * 64, ctx * TOK) - at(plane, zz, 0) * TOK
+        key = lax.broadcasted_iota(jnp.int32, (ROW, COLS), 0)
+
         def hide(s):
-            if not causal:
-                return s
-            key = at(plane, zz, 0) * TOK + lax.broadcasted_iota(jnp.int32, (ROW, COLS), 0)
-            return jnp.where(key <= ctx * TOK + token, s, HIDDEN)
+            return jnp.where(key <= token + offset, s, HIDDEN)
 
         attend(slot, row(0, plane, zz), row(1, plane, zz), hide)
 
     def attend_panels():
         reset(3)
-        for h in range(GROUP):
-            qs[3, pl.ds(h * TOK, TOK)] = q_cross[:, h * HEAD : (h + 1) * HEAD]
+        wait_queries(3, 4)
         for d in (1, 2, 3):
             s_wait(d)
         before = (y == 0) & (bundle > 0)
@@ -290,101 +333,138 @@
     for kind in range(2):
         z_copy(kind, 1).start()
         z_copy(kind, 2).start()
-    part1(0)
+    keys_out(0)
+    values_out(0)
     for d in range(1, 8):
         p_copy(d).start()
-    for kind in range(2):
-        z_copy(kind, 3).start()
-
-    @pl.when(x >= 2)
+    wait_queries(0, 3)
+
+    @pl.when(x == 3)
     def _():
         q_copy().start()
 
     pan[y, tp] = staged[tp]
-    reset(0)
-
-    @pl.when(x == 0)
-    def _():
-        reset(1)
-        reset(2)
-
-    part2(0)
-    for d in range(1, 8):
-        p_wait(d)
-    for d in (1, 2, 3):
-        s_copy(d).start()
-
-    @pl.when(bundle < 15)
-    def _():
-        next_copy().start()
-
-    part3(0)
-    part1(1)
-
-    def turn(zi, _):
+    spread(0, 2)
+    spread(0, 3)
+    rows_out(0)
+    own_onward(0)
+    onward(0)
+    keys_out(1)
+    keys_out(2)
+
+    def ahead(t):
+        @pl.when(t == 1)
+        def _():
+            spread(1, 2)
+            spread(2, 2)
+            values_out(1)
+            values_out(2)
+
+            @pl.when(x == 2)
+            def _():
+                q_copy().start()
+
+            panels_out()
+
+        @pl.when(t == 2)
+        def _():
+            keys_out(3)
+            for zi in (1, 2):
+                spread(zi, 3)
+            for zi in (1, 2):
+                own_onward(zi)
+            for zi in (1, 2):
+                rows_out(zi)
+
+        @pl.when(t == 3)
+        def _():
+            values_out(3)
+            onward(1)
+            onward(2)
+
+        @pl.when(t == 4)
+        def _():
+            spread(3, 2)
+
+        @pl.when(t == 5)
+        def _():
+            spread(3, 3)
+            rows_out(3)
+            own_onward(3)
+
+        @pl.when(t == 6)
+        def _():
+            onward(3)
+
+        @pl.when(t == 9)
+        def _():
+            attend_panels()
+
+    def give_back(slot):
+        upper = lax.broadcasted_iota(jnp.int32, (8, COLS), 0) < 4
+        total = jnp.sum(tot[slot], axis=0, keepdims=True)
+        part_out[slot - 1] = (acc[slot] * (1.0 / total)).astype(BF16)
+        stat_out[slot - 1] = jnp.where(upper, top[slot], total)
+        for copy in o_copies(slot):
+            copy.start()
+
+    def turn(t, code):
+        zi, j = code[0] % 4, code[1] % 4
         zz = origin(zi)
-
-        @pl.when(zi < 3)
-        def _():
-            part2(zi + 1)
-
-        y_wait(zi, 0, 2)
-
-        @pl.when(zz <= z)
-        def _():
-            attend_row(0, x, zz, True)
-
-        @pl.when(zi < 2)
-        def _():
-            part1(zi + 2)
-
-        part4(zi)
-
-        @pl.when(zi < 3)
-        def _():
-            part3(zi + 1)
-
-        @pl.when(x > 0)
+        ahead(t)
+
+        @pl.when((x == 0) & (t == 1))
+        def _():
+            q_wait(2)
+
+        @pl.when((x == 0) & (t == 4))
+        def _():
+            q_wait(1)
+
+        @pl.when((x > 0) & (j == 0))
+        def _():
+            y_wait(zi, 0, 2)
+
+        @pl.when((x == 0) & ((t == 0) | (t == 2) | (t == 3) | (t == 7)))
+        def _():
+            y_wait(zi, 0, 2)
+
+        @pl.when((x > 0) & (j == 1))
         def _():
             y_wait(zi, 2, 2)
+
+        @pl.when(((x == 1) | (x == 2)) & (j == 1))
+        def _():
             y_wait(zi, 3, 2)
 
-        @pl.when(x == 3)
+        @pl.when((x == 3) & (j == 1))
         def _():
             row_wait(zi, 2, 0)
 
-        @pl.when((x == 0) & (zi == 0))
-        def _():
-            q_wait(1)
-            q_wait(2)
-
-        attend_row(jnp.where(x == 0, 1, 0), jnp.where(x == 0, 0, x - 1), zz, False)
-
-        @pl.when(x == 3)
-        def _():
+        @pl.when((x == 3) & (j == 2))
+        def _():
+            y_wait(zi, 3, 2)
             row_wait(zi, 1, 1)
 
-        @pl.when((x == 0) | (x == 3))
-        def _():
-            attend_row(jnp.where(x == 0, 2, 0), jnp.where(x == 0, 0, 1), zz, False)
-
-        @pl.when(zi == 0)
-        def _():
-            attend_panels()
-
-        return 0
-
-    lax.fori_loop(0, 4, turn, 0)
-
-    @pl.when(x == 0)
-    def _():
-        upper = lax.broadcasted_iota(jnp.int32, (8, COLS), 0) < 4
-        for slot in (1, 2):
-            total = jnp.sum(tot[slot], axis=0, keepdims=True)
-            part_out[slot - 1] = (acc[slot] * (1.0 / total)).astype(BF16)
-            stat_out[slot - 1] = jnp.where(upper, top[slot], total)
-            for copy in o_copies(slot):
-                copy.start()
+        @pl.when(jnp.where(j == 0, zz <= z, (j == 1) | (x == 0) | (x == 3)))
+        def _():
+            attend_row(jnp.where(x == 0, j, 0), jnp.where(x == 0, 0, x - j), zz)
+
+        for when, slot in ((7, 2), (8, 1)):
+
+            @pl.when((x == 0) & (t == when))
+            def _(slot=slot):
+                give_back(slot)
+
+        return code[0] // 4, code[1] // 4
+
+    def digits(values):
+        return sum(v * 4**k for k, v in enumerate(values))
+
+    first = [[0, 0, 1, 2, 0, 1, 2, 3, 3, 1, 2, 3], [0, 2, 2, 2, 1, 1, 1, 2, 1, 0, 0, 0]]
+    others = [[0, 0, 0, 1, 2, 1, 2, 1, 2, 3, 3, 3], [0, 1, 2, 0, 0, 1, 1, 2, 2, 0, 1, 2]]
+    plan = tuple(jnp.where(x == 0, digits(a), digits(b)) for a, b in zip(first, others))
+    lax.fori_loop(0, 12, turn, plan)
 
     @pl.when(x >= 2)
     def _():
@@ -404,9 +484,11 @@
         c = slice(h * TOK, (h + 1) * TOK)
         self_out[:, h * HEAD : (h + 1) * HEAD] = (acc[0, :, c] * inverse[:, c]).T.astype(BF16)
 
+    for kind in range(2):
+        for d in (1, 2):
+            z_copy(kind, d).wait_send()
+            z_onward(kind, d - 1).wait_send()
     for d in (1, 2, 3):
-        for kind in range(2):
-            z_copy(kind, d).wait_send()
         s_copy(d).wait_send()
     for d in range(1, 8):
         p_copy(d).wait_send()
@@ -429,7 +511,6 @@
         @pl.when(x < 3)
         def _():
             x_copy(zi, 0, 2, None).wait_send()
-            row_copy(zi, 1, 3, 1).wait_send()
 
         @pl.when(x < 2)
         def _():
@@ -438,6 +519,10 @@
         @pl.when(x == 1)
         def _():
             x_copy(zi, 0, 3, 3).wait_send()
+
+        @pl.when((x == 1) | (x == 2))
+        def _():
+            row_copy(zi).wait_send()
 
         return 0
 
@@ -457,12 +542,13 @@
 def local(query_self, key_value_self, query_cross, panels, image_span, panel_image, cross_gate):
     smem = pl.BlockSpec(memory_space=pltpu.SMEM)
     vmem = pl.BlockSpec(memory_space=pltpu.VMEM)
+    hbm = pl.BlockSpec(memory_space=pltpu.HBM)
     dma = pltpu.SemaphoreType.DMA
     shape = jax.ShapeDtypeStruct((TOK, COLS), BF16)
     return pl.pallas_call(
         kernel,
         out_shape=(shape, shape),
-        in_specs=[smem] * 3 + [vmem] * 4,
+        in_specs=[smem] * 3 + [hbm] * 4,
         out_specs=(vmem, vmem),
         scratch_shapes=[
             pltpu.VMEM((4, COLS, HEAD), BF16),
@@ -484,6 +570,7 @@
             dma((2, 2)), dma((2,)),
             dma((8,)), dma((8,)),
             dma((4,)), dma((8,)),
+            pltpu.VMEM((2, 1, 8, COLS), BF16), dma((5,)),
         ],
         compiler_params=pltpu.CompilerParams(
             collective_id=0, has_side_effects=True, vmem_limit_bytes=48 << 20

time: 66.6 us -> 58.2 us (0.87)
  the two profiles are of different devices: /device:TPU:70 before, /device:TPU:6 now
where the time goes in v2:
time: 58.2 us; the launch traced here: 57.9 us
  Pallas kernels  51.7 us (89%)
  local copies, waits for them, and re-layouts  4.82 us (8%)
  between operations  1.36 us (2%)
    pallas_call x1, Pallas kernels, local(): pl.pallas_call(kernel, out_shape=(shape, shape), in_specs=[smem] * 3 + [h...  51.7 us
    unnamed x15, local copies, waits for them, and re-layouts  4.68 us

profile of v2, /device:TPU:6, one launch (start us, length us, event | category | flops | bytes accessed | tf_op | source)
XLA Modules:
  0.0 57.9 jit_solution(12437167347158641161)
XLA Ops:
  0.6 0.0 copy-start.5
  0.6 0.0 copy-start.2
  1.3 0.0 copy-done.5
  1.3 0.1 copy.10
  1.4 0.0 copy-start.4
  1.4 0.1 reshape.7.span
  1.6 0.0 copy-done.2
  1.6 0.5 copy-done.4
  2.1 0.0 copy-start
  2.1 0.9 %copy-done = bf16[128,1024]{1,0:T(8,128)(2,1)S(1)} copy-done((bf16[128,1024]{1,0:T(8,128)(2,1)S(1)}, bf16[128,1024]{1,0:T(8,128)(2,1)}, u32[]{:S(2)}) %copy-start) | copy-done | bytes 262168
  3.0 0.0 copy-start.1
  3.1 0.9 %copy-done.1 = bf16[128,1024]{1,0:T(8,128)(2,1)S(1)} copy-done((bf16[128,1024]{1,0:T(8,128)(2,1)S(1)}, bf16[128,1024]{1,0:T(8,128)(2,1)}, u32[]{:S(2)}) %copy-start.1) | copy-done | bytes 262168
  4.0 0.0 copy-start.3
  4.0 0.8 %copy-done.3 = bf16[2,1,8,1024]{3,2,1,0:T(8,128)(2,1)S(1)} copy-done((bf16[2,1,8,1024]{3,2,1,0:T(8,128)(2,1)S(1)}, bf16[2,1,8,1024]{3,2,1,0:T(8,128)(2,1)}, u32[]{:S(2)}) %copy-start.3) | copy-done | bytes 32792
  4.8 51.7 %attention.1 = (bf16[128,1024]{1,0:T(8,128)(2,1)S(1)}, bf16[128,1024]{1,0:T(8,128)(2,1)S(1)}) custom-call(s32[128]{0:T(128)S(1)} %reshape.7.span, s32[64]{0:T(128)S(1)} %copy-done.4, f32[1]{0:T(128)S(6)} %copy.13.gate, bf16[128,1024]{1,0:T(8,128)(2,1)S(1)} %copy-done, bf16[2,128,128]{2,1,0:T(8,128)(2,1)S(1)} %copy-done.2, bf16[128,1024]{1,0:T(8,128)(2,1)S(1)} %copy-done.1, ...), custom_call_target="tpu_custom_call" | custom-call | tf_op jit(solution)/shard_map/attention/pallas_call | solution.py:548
  56.5 0.7 %copy.14 = bf16[128,1024]{1,0:T(8,128)(2,1)} copy(bf16[128,1024]{1,0:T(8,128)(2,1)S(1)} %get-tuple-element.4) | data formatting | bytes 524288
  57.2 0.7 %copy.15 = bf16[128,1024]{1,0:T(8,128)(2,1)} copy(bf16[128,1024]{1,0:T(8,128)(2,1)S(1)} %get-tuple-element.5) | data formatting | bytes 524288
Async XLA Ops:
  0.6 0.7 %copy-start.5 = (s32[64,2]{0,1:T(2,128)S(1)}, s32[64,2]{0,1:T(2,128)}, u32[]{:S(2)}) copy-start(s32[64,2]{0,1:T(2,128)} %param.11) | copy-start | bytes 1540
  0.6 0.9 %copy-start.2 = (bf16[2,128,128]{2,1,0:T(8,128)(2,1)S(1)}, bf16[2,128,128]{2,1,0:T(8,128)(2,1)}, u32[]{:S(2)}) copy-start(bf16[2,128,128]{2,1,0:T(8,128)(2,1)} %kv_own.1) | copy-start | bytes 196612
  1.4 0.7 %copy-start.4 = (s32[64]{0:T(128)S(1)}, s32[64]{0:T(128)}, u32[]{:S(2)}) copy-start(s32[64]{0:T(128)} %slot_image.1) | copy-start | bytes 772
  2.1 0.9 %copy-start = (bf16[128,1024]{1,0:T(8,128)(2,1)S(1)}, bf16[128,1024]{1,0:T(8,128)(2,1)}, u32[]{:S(2)}) copy-start(bf16[128,1024]{1,0:T(8,128)(2,1)} %q_self.1) | copy-start | bytes 786436
  3.0 0.9 %copy-start.1 = (bf16[128,1024]{1,0:T(8,128)(2,1)S(1)}, bf16[128,1024]{1,0:T(8,128)(2,1)}, u32[]{:S(2)}) copy-start(bf16[128,1024]{1,0:T(8,128)(2,1)} %q_cross.1) | copy-start | bytes 786436
  4.0 0.8 %copy-start.3 = (bf16[2,1,8,1024]{3,2,1,0:T(8,128)(2,1)S(1)}, bf16[2,1,8,1024]{3,2,1,0:T(8,128)(2,1)}, u32[]{:S(2)}) copy-start(bf16[2,1,8,1024]{3,2,1,0:T(8,128)(2,1)} %panels.1) | copy-start | bytes 98308

commit v3 on v2

--- a/solution.py
+++ b/solution.py
@@ -96,10 +96,10 @@
         copy.wait()
     pl.semaphore_wait(barrier, jnp.where(bundle < 15, 17, 16))
 
-    def z_copy(kind, d):
-        target = (z + {1: 1, 2: 3}[d]) % 4
+    def z_copy(kind, zi):
+        target = (z + (0, 1, 3)[zi]) % 4
         block = kv.at[kind, ctx]
-        return remote(block, block, z_send.at[d, kind], z_recv.at[d, kind], (at(x, target, y), tp))
+        return remote(block, block, z_send.at[zi, kind], z_recv.at[zi, kind], (at(x, target, y), tp))
 
     def z_half(kind, zz, half):
         return kv.at[kind, at(x, zz, y), pl.ds(half * 64, 64)]
@@ -121,50 +121,40 @@
             remote(block, block, z_send.at[0, 0], z_recv.at[3 * half, kind], aside).wait_recv()
 
     def item(i):
-        if i < 2:
-            return i, x
-        if i == 2:
-            return 0, x - 1
-        return jnp.where(x == 3, 0, 1), jnp.where(x == 3, 1, x - 1)
-
-    def y_copy(zi, i, way, yy):
+        return (0, x) if i == 0 else (1, (x, x, x - 1, 1)[i])
+
+    def y_copy(zi, i, way):
         kind, plane = item(i)
-        to = {0: (y + 1) % 4, 1: (y + 3) % 4, 2: (y + 2) % 4}[way]
-        block = kv.at[kind, at(plane, origin(zi), yy)]
+        to = (y + (1, 3, 2)[way]) % 4
+        block = kv.at[kind, at(plane, origin(zi), y)]
         return remote(block, block, y_send.at[zi, i, way], y_recv.at[zi, i, way], (at(x, z, to), tp))
-
-    def y_onward(zi, i):
-        kind, plane = item(i)
-        up = i != 2
-        from_y = (y + 3) % 4 if up else (y + 1) % 4
-        to = (y + 1) % 4 if up else (y + 3) % 4
-        block = kv.at[kind, at(plane, origin(zi), from_y)]
-        return remote(block, block, y_send.at[zi, i, 2], y_recv.at[zi, i, 2], (at(x, z, to), tp))
 
     def y_wait(zi, i, way):
         kind, plane = item(i)
-        yy = {0: (y + 3) % 4, 1: (y + 1) % 4, 2: (y + 2) % 4}[way]
+        yy = (y + (3, 1, 2)[way]) % 4
         block = kv.at[kind, at(plane, origin(zi), yy)]
         remote(block, block, z_send.at[0, 0], y_recv.at[zi, i, way], (ctx, (tp + 1) % 8)).wait_recv()
 
-    def x_copy(zi, kind, i, plane):
-        block = kv.at[kind, at(x, origin(zi), y)]
-        lane = kind if plane is None else 2
-        to = x + 1 if plane is None else plane
-        return remote(block, block, x_send.at[zi, lane], x_recv.at[zi, i], (at(to, z, y), tp))
+    def x_copy(zi, i):
+        block = kv.at[1, at(x, origin(zi), y)]
+        to = (at(x + 1 if i == 2 else 3, z, y), tp)
+        return remote(block, block, x_send.at[zi, i - 2], x_recv.at[zi, i - 2], to)
 
     def x_wait(zi, i):
         kind, plane = item(i)
         block = kv.at[kind, at(plane, origin(zi), y)]
-        remote(block, block, z_send.at[0, 0], x_recv.at[zi, i], (ctx, (tp + 1) % 8)).wait_recv()
-
-    def row_copy(zi):
-        rows = kv.at[1, pl.ds(at(x, origin(zi), 0), 4)]
-        return remote(rows, rows, r_send.at[zi], r_recv.at[zi, 2 - x], (at(3, z, y), tp))
-
-    def row_wait(zi, plane, slot):
-        rows = kv.at[1, pl.ds(at(plane, origin(zi), 0), 4)]
-        remote(rows, rows, z_send.at[0, 0], r_recv.at[zi, slot], (ctx, (tp + 1) % 8)).wait_recv()
+        aside = (ctx, (tp + 1) % 8)
+        remote(block, block, z_send.at[0, 0], x_recv.at[zi, i - 2], aside).wait_recv()
+
+    def row_copy(kind, zi, far):
+        rows = kv.at[kind, pl.ds(at(x, origin(zi), 0), 4)]
+        to = (at(3 if far else x + 1, z, y), tp)
+        return remote(rows, rows, r_send.at[kind, zi, far], r_recv.at[kind, zi, far], to)
+
+    def row_wait(kind, zi, far):
+        rows = kv.at[kind, pl.ds(at(1 if far else x - 1, origin(zi), 0), 4)]
+        aside = (ctx, (tp + 1) % 8)
+        remote(rows, rows, z_send.at[0, 0], r_recv.at[kind, zi, far], aside).wait_recv()
 
     def q_copy():
         return remote(qs.at[0], qs.at[x - 1], q_send, q_recv.at[x - 1], (at(0, z, y), tp))
@@ -201,65 +191,50 @@
         block = pan.at[4 + d]
         remote(block, block, s_send.at[0], s_recv.at[4 + d], (ctx, (tp + 1) % 8)).wait_recv()
 
-    def keys_out(zi):
+    def block_out(kind, zi):
         if zi > 0:
-            z_wait(0, zi)
+            z_wait(kind, zi)
         if zi in (1, 2):
-            z_onward(0, zi - 1).start()
+            z_onward(kind, zi - 1).start()
+        if kind == 1 and zi != 1:
+
+            @pl.when(x < 3)
+            def _():
+                x_copy(zi, 2).start()
+
+            @pl.when(x == 1)
+            def _():
+                x_copy(zi, 3).start()
+
+        for way in range(3):
+            y_copy(zi, kind, way).start()
+
+    def row_there(kind, zi):
+        for way in range(3):
+            y_wait(zi, kind, way)
+
+    def rows_out(kind, zi):
+        row_there(kind, zi)
 
         @pl.when(x < 3)
         def _():
-            x_copy(zi, 0, 2, None).start()
+            row_copy(kind, zi, 0).start()
 
         @pl.when(x == 1)
         def _():
-            x_copy(zi, 0, 3, 3).start()
-
-        y_copy(zi, 0, 0, y).start()
-        y_copy(zi, 0, 1, y).start()
-
-    def values_out(zi):
-        if zi > 0:
-            z_wait(1, zi)
-        if zi in (1, 2):
-            z_onward(1, zi - 1).start()
-
-        @pl.when(x < 2)
-        def _():
-            x_copy(zi, 1, 3, None).start()
-
-        for way in range(3):
-            y_copy(zi, 1, way, y).start()
-
-    def spread(zi, i):
-        @pl.when(x > 0)
-        def _():
-            x_wait(zi, i)
-            y_copy(zi, i, 0, y).start()
-            y_copy(zi, i, 1, y).start()
-
-    def rows_out(zi):
-        for way in range(3):
-            y_wait(zi, 1, way)
-
-        @pl.when((x == 1) | (x == 2))
-        def _():
-            row_copy(zi).start()
-
-    def own_onward(zi):
-        y_wait(zi, 0, 0)
-        y_onward(zi, 0).start()
-        y_wait(zi, 0, 1)
-
-    def onward(zi):
-        @pl.when(x > 0)
-        def _():
-            y_wait(zi, 2, 1)
-            y_onward(zi, 2).start()
-            y_wait(zi, 2, 0)
-            y_wait(zi, 3, 0)
-            y_onward(zi, 3).start()
-            y_wait(zi, 3, 1)
+            row_copy(kind, zi, 1).start()
+
+    def items():
+        return (2, x > 0), (3, x == 3)
+
+    def spread(zi):
+        for i, there in items():
+
+            @pl.when(there)
+            def _(i=i):
+                x_wait(zi, i)
+                for way in range(3):
+                    y_copy(zi, i, way).start()
 
     def panels_out():
         for d in range(1, 8):
@@ -289,14 +264,21 @@
 
     token = lax.broadcasted_iota(jnp.int32, (1, COLS), 1) % TOK
 
-    def attend_row(slot, plane, zz):
-        offset = jnp.where(slot > 0, TOK * 64, ctx * TOK) - at(plane, zz, 0) * TOK
+    def attend_rows(slot, rows, causal):
+        first = jnp.where(slot > 0, TOK * 64, ctx * TOK)
         key = lax.broadcasted_iota(jnp.int32, (ROW, COLS), 0)
 
         def hide(s):
-            return jnp.where(key <= token + offset, s, HIDDEN)
-
-        attend(slot, row(0, plane, zz), row(1, plane, zz), hide)
+            if not causal:
+                return s
+            parts = []
+            for k, (plane, zz) in enumerate(rows):
+                seen = key <= token + (first - at(plane, zz, 0) * TOK)
+                parts.append(jnp.where(seen, s[k * ROW : (k + 1) * ROW], HIDDEN))
+            return jnp.concatenate(parts, axis=0)
+
+        keys, values = [jnp.concatenate([row(k, *r) for r in rows], axis=0) for k in (0, 1)]
+        attend(slot, keys, values, hide)
 
     def attend_panels():
         reset(3)
@@ -318,7 +300,7 @@
             masks = []
             for k in range(4):
                 image = slot_image[(bundle - which) * 4 + k]
-                reads = (here >= span[image * 2]) & (here < span[image * 2 + 1])
+                reads = (here >= span[0, image]) & (here < span[1, image])
                 masks.append(jnp.broadcast_to(jnp.where(reads, 0.0, HIDDEN), (64, COLS)))
             mask = jnp.concatenate(masks, axis=0)
             attend(3, keys, values, lambda s: s + mask)
@@ -331,72 +313,48 @@
             cross_out[:, h * HEAD : (h + 1) * HEAD] = (acc[3, :, c] * factor[:, c]).T.astype(BF16)
 
     for kind in range(2):
-        z_copy(kind, 1).start()
-        z_copy(kind, 2).start()
-    keys_out(0)
-    values_out(0)
+        for zi in (1, 2):
+            z_copy(kind, zi).start()
+    for kind in range(2):
+        block_out(kind, 0)
     for d in range(1, 8):
         p_copy(d).start()
     wait_queries(0, 3)
 
-    @pl.when(x == 3)
+    @pl.when(x >= 2)
     def _():
         q_copy().start()
 
     pan[y, tp] = staged[tp]
-    spread(0, 2)
-    spread(0, 3)
-    rows_out(0)
-    own_onward(0)
-    onward(0)
-    keys_out(1)
-    keys_out(2)
+    rows_out(0, 0)
+    spread(0)
+    row_there(1, 0)
 
     def ahead(t):
         @pl.when(t == 1)
         def _():
-            spread(1, 2)
-            spread(2, 2)
-            values_out(1)
-            values_out(2)
-
-            @pl.when(x == 2)
-            def _():
-                q_copy().start()
+            for zi in (1, 2):
+                block_out(0, zi)
 
             panels_out()
+            for zi in (1, 2):
+                block_out(1, zi)
+            rows_out(0, 1)
+            block_out(0, 3)
+            rows_out(0, 2)
+            spread(2)
 
         @pl.when(t == 2)
         def _():
-            keys_out(3)
-            for zi in (1, 2):
-                spread(zi, 3)
-            for zi in (1, 2):
-                own_onward(zi)
-            for zi in (1, 2):
-                rows_out(zi)
+            block_out(1, 3)
+            rows_out(1, 1)
 
         @pl.when(t == 3)
         def _():
-            values_out(3)
-            onward(1)
-            onward(2)
-
-        @pl.when(t == 4)
-        def _():
-            spread(3, 2)
-
-        @pl.when(t == 5)
-        def _():
-            spread(3, 3)
-            rows_out(3)
-            own_onward(3)
-
-        @pl.when(t == 6)
-        def _():
-            onward(3)
-
-        @pl.when(t == 9)
+            rows_out(0, 3)
+            spread(3)
+
+        @pl.when(t == jnp.where(x == 0, 6, 3))
         def _():
             attend_panels()
 
@@ -408,9 +366,25 @@
         for copy in o_copies(slot):
             copy.start()
 
+    def first_use(zi, j):
+        @pl.when(j == 0)
+        def _():
+            if zi > 1:
+                row_there(1, zi)
+
+        for k, there in ((1, x > 0), (2, x == 3)):
+
+            @pl.when((j == k) & there)
+            def _(k=k):
+                row_wait(0, zi, k - 1)
+                if zi == 1:
+                    row_wait(1, zi, k - 1)
+                else:
+                    for way in range(3):
+                        y_wait(zi, k + 1, way)
+
     def turn(t, code):
-        zi, j = code[0] % 4, code[1] % 4
-        zz = origin(zi)
+        step, zi, j = (c % 8 for c in code)
         ahead(t)
 
         @pl.when((x == 0) & (t == 1))
@@ -421,50 +395,52 @@
         def _():
             q_wait(1)
 
-        @pl.when((x > 0) & (j == 0))
-        def _():
-            y_wait(zi, 0, 2)
-
-        @pl.when((x == 0) & ((t == 0) | (t == 2) | (t == 3) | (t == 7)))
-        def _():
-            y_wait(zi, 0, 2)
-
-        @pl.when((x > 0) & (j == 1))
-        def _():
-            y_wait(zi, 2, 2)
-
-        @pl.when(((x == 1) | (x == 2)) & (j == 1))
-        def _():
-            y_wait(zi, 3, 2)
-
-        @pl.when((x == 3) & (j == 1))
-        def _():
-            row_wait(zi, 2, 0)
-
-        @pl.when((x == 3) & (j == 2))
-        def _():
-            y_wait(zi, 3, 2)
-            row_wait(zi, 1, 1)
-
-        @pl.when(jnp.where(j == 0, zz <= z, (j == 1) | (x == 0) | (x == 3)))
-        def _():
-            attend_row(jnp.where(x == 0, j, 0), jnp.where(x == 0, 0, x - j), zz)
-
-        for when, slot in ((7, 2), (8, 1)):
+        slot = jnp.where(x == 0, j, 0)
+        plane = jnp.where(x == 0, 0, x - j)
+        both = (step == 3) & (x == 3)
+        fresh = (step > 0) & ((x > 0) | (t < 4))
+        wait_j = jnp.where(x == 0, 0, j)
+        for k in range(4):
+            hit = (zi == k) if k in (0, 3) else (zi == k) | (step == 2)
+
+            @pl.when(hit & fresh)
+            def _(k=k):
+                first_use(k, wait_j)
+                pl.when(both)(lambda: first_use(k, 2))
+
+        single, below, above, far = origin(zi), origin(1), origin(2), origin(3)
+
+        @pl.when(((step == 1) & ((j > 0) | (single <= z))) | ((step == 3) & (x < 3)))
+        def _():
+            attend_rows(slot, ((plane, single),), True)
+
+        @pl.when((step == 2) & (j == 0) & (z > 0))
+        def _():
+            attend_rows(slot, ((plane, below), (plane, above)), True)
+
+        @pl.when(((step == 2) & (j > 0)) | both | (step == 4))
+        def _():
+            one = jnp.where(step == 2, below, jnp.where(step == 3, single, z))
+            two = jnp.where(step == 2, above, jnp.where(step == 3, single, far))
+            attend_rows(slot, ((plane, one), (jnp.where(step == 3, plane - 1, plane), two)), False)
+
+        for when, slot_out in ((3, 2), (5, 1)):
 
             @pl.when((x == 0) & (t == when))
-            def _(slot=slot):
-                give_back(slot)
-
-        return code[0] // 4, code[1] // 4
+            def _(slot_out=slot_out):
+                give_back(slot_out)
+
+        return tuple(c // 8 for c in code)
 
     def digits(values):
-        return sum(v * 4**k for k, v in enumerate(values))
-
-    first = [[0, 0, 1, 2, 0, 1, 2, 3, 3, 1, 2, 3], [0, 2, 2, 2, 1, 1, 1, 2, 1, 0, 0, 0]]
-    others = [[0, 0, 0, 1, 2, 1, 2, 1, 2, 3, 3, 3], [0, 1, 2, 0, 0, 1, 1, 2, 2, 0, 1, 2]]
-    plan = tuple(jnp.where(x == 0, digits(a), digits(b)) for a, b in zip(first, others))
-    lax.fori_loop(0, 12, turn, plan)
+        return sum(v * 8**k for k, v in enumerate(values))
+
+    first = "11212421", "00131013", "02221100"
+    others = "13231330", "00123130", "01010110"
+    plan = tuple(
+        jnp.where(x == 0, digits(map(int, a)), digits(map(int, b))) for a, b in zip(first, others)
+    )
+    lax.fori_loop(0, 8, turn, plan)
 
     @pl.when(x >= 2)
     def _():
@@ -485,9 +461,9 @@
         self_out[:, h * HEAD : (h + 1) * HEAD] = (acc[0, :, c] * inverse[:, c]).T.astype(BF16)
 
     for kind in range(2):
-        for d in (1, 2):
-            z_copy(kind, d).wait_send()
-            z_onward(kind, d - 1).wait_send()
+        for zi in (1, 2):
+            z_copy(kind, zi).wait_send()
+            z_onward(kind, zi - 1).wait_send()
     for d in (1, 2, 3):
         s_copy(d).wait_send()
     for d in range(1, 8):
@@ -497,36 +473,33 @@
     def _():
         next_copy().wait_send()
 
-    def drain(zi, _):
+    for zi in range(4):
         for i in (0, 1):
             for way in range(3):
-                y_copy(zi, i, way, y).wait_send()
-
-        @pl.when(x > 0)
-        def _():
-            for i in (2, 3):
-                for way in range(3):
-                    y_copy(zi, i, way, y).wait_send()
+                y_copy(zi, i, way).wait_send()
+        if zi != 1:
+            for i, there in items():
+
+                @pl.when(there)
+                def _(i=i, zi=zi):
+                    for way in range(3):
+                        y_copy(zi, i, way).wait_send()
 
         @pl.when(x < 3)
-        def _():
-            x_copy(zi, 0, 2, None).wait_send()
-
-        @pl.when(x < 2)
-        def _():
-            x_copy(zi, 1, 3, None).wait_send()
+        def _(zi=zi):
+            row_copy(0, zi, 0).wait_send()
+            if zi == 1:
+                row_copy(1, zi, 0).wait_send()
+            else:
+                x_copy(zi, 2).wait_send()
 
         @pl.when(x == 1)
-        def _():
-            x_copy(zi, 0, 3, 3).wait_send()
-
-        @pl.when((x == 1) | (x == 2))
-        def _():
-            row_copy(zi).wait_send()
-
-        return 0
-
-    lax.fori_loop(0, 4, drain, 0)
+        def _(zi=zi):
+            row_copy(0, zi, 1).wait_send()
+            if zi == 1:
+                row_copy(1, zi, 1).wait_send()
+            else:
+                x_copy(zi, 3).wait_send()
 
     @pl.when(x >= 2)
     def _():
@@ -563,9 +536,9 @@
             pltpu.VMEM((2, 8, COLS), F32),
             pltpu.VMEM((8, COLS), F32),
             dma((4, 2)), dma((4, 2)),
-            dma((4, 3)), dma((4, 4)),
+            dma((4, 2)), dma((4, 2)),
             dma((4, 4, 3)), dma((4, 4, 3)),
-            dma((4,)), dma((4, 2)),
+            dma((2, 4, 2)), dma((2, 4, 2)),
             dma, dma((3,)),
             dma((2, 2)), dma((2,)),
             dma((8,)), dma((8,)),
@@ -573,10 +546,10 @@
             pltpu.VMEM((2, 1, 8, COLS), BF16), dma((5,)),
         ],
         compiler_params=pltpu.CompilerParams(
-            collective_id=0, has_side_effects=True, vmem_limit_bytes=48 << 20
+            collective_id=0, has_side_effects=True, vmem_limit_bytes=64 << 20
         ),
         name="attention",
-    )(image_span.reshape(-1), panel_image, cross_gate, query_self, key_value_self, query_cross, panels)
+    )(image_span.T, panel_image, cross_gate, query_self, key_value_self, query_cross, panels)
 
 
 def solution(mesh):

time: 58.2 us -> 54.4 us (0.935)
  the two profiles are of different devices: /device:TPU:6 before, /device:TPU:4 now
where the time goes in v3:
time: 54.4 us; the launch traced here: 54.2 us
  Pallas kernels  50.5 us (93%)
  local copies, waits for them, and re-layouts  2.42 us (4%)
  between operations  1.3 us (2%)
    pallas_call x1, Pallas kernels, local(): pl.pallas_call(kernel, out_shape=(shape, shape), in_specs=[smem] * 3 + [h...  50.5 us
    unnamed x4, local copies, waits for them, and re-layouts  2.42 us

profile of v3, /device:TPU:4, one launch (start us, length us, event | category | flops | bytes accessed | tf_op | source)
XLA Modules:
  0.0 54.2 jit_solution(4613991616871483752)
XLA Ops:
  1.3 50.5 %attention.1 = (bf16[128,1024]{1,0:T(8,128)(2,1)}, bf16[128,1024]{1,0:T(8,128)(2,1)}) custom-call(s32[2,64]{1,0:T(2,128)} %bitcast.1, s32[64]{0:T(128)} %slot_image.1, f32[1]{0:T(128)S(6)} %copy.11.gate, bf16[128,1024]{1,0:T(8,128)(2,1)} %q_self.1, bf16[2,128,128]{2,1,0:T(8,128)(2,1)} %kv_own.1, bf16[128,1024]{1,0:T(8,128)(2,1)} %q_cross.1, ...), custom_call_target="tpu_custom_call" | custom-call | tf_op jit(solution)/shard_map/attention/pallas_call | solution.py:521
  51.7 0.0 copy-start
  51.8 1.7 %copy.12 = bf16[128,1024]{1,0:T(8,128)(2,1)} copy(bf16[128,1024]{1,0:T(8,128)(2,1)} %get-tuple-element.4) | data formatting | bytes 524288
  53.5 0.0 copy-done
  53.5 0.7 %copy.13 = bf16[128,1024]{1,0:T(8,128)(2,1)} copy(bf16[128,1024]{1,0:T(8,128)(2,1)S(1)} %copy-done) | data formatting | bytes 524288
Async XLA Ops:
  51.7 1.7 %copy-start = (bf16[128,1024]{1,0:T(8,128)(2,1)S(1)}, bf16[128,1024]{1,0:T(8,128)(2,1)}, u32[]{:S(2)}) copy-start(bf16[128,1024]{1,0:T(8,128)(2,1)} %get-tuple-element.5) | copy-start | bytes 786436

commit v4 on v3

--- a/solution.py
+++ b/solution.py
@@ -26,7 +26,7 @@
     span, slot_image, gate, q_self, kv_own, q_cross, panels, self_out, cross_out,
     qs, kv, staged, pan, acc, top, tot, part_out, part_in, stat_out, stat_in,
     z_send, z_recv, x_send, x_recv, y_send, y_recv, r_send, r_recv,
-    q_send, q_recv, o_send, o_recv, p_send, p_recv, s_send, s_recv, panel_in, in_sem,
+    q_send, q_recv, o_send, o_recv, p_send, p_recv, s_send, s_recv, panel_in, in_sem, result, out_sem,
 ):
     ctx = lax.axis_index("ctx")
     tp = lax.axis_index("tp")
@@ -79,18 +79,6 @@
 
     def wait_queries(slot, sem):
         pltpu.make_async_copy(qs.at[slot], qs.at[slot], in_sem.at[sem]).wait()
-
-    reset(0)
-
-    @pl.when(x == 0)
-    def _():
-        reset(1)
-        reset(2)
-
-    own_panel.wait()
-    pair = jnp.concatenate([panel_in[0, 0].astype(F32), panel_in[1, 0].astype(F32)], axis=0)
-    for h in range(GROUP):
-        staged[h] = pair[:, h * HEAD : (h + 1) * HEAD].astype(BF16)
 
     for copy in own_kv:
         copy.wait()
@@ -121,7 +109,16 @@
             remote(block, block, z_send.at[0, 0], z_recv.at[3 * half, kind], aside).wait_recv()
 
     def item(i):
-        return (0, x) if i == 0 else (1, (x, x, x - 1, 1)[i])
+        return (i, x) if i < 2 else (1, x + 1 - i)
+
+    def senders(far):
+        return x == 1 if far else x < 3
+
+    def receivers(far):
+        return x == 3 if far else x > 0
+
+    def rows_over(kind, zi, plane, far):
+        return True if kind == 0 else (plane == 3) & (far == 0 and zi in (1, 2))
 
     def y_copy(zi, i, way):
         kind, plane = item(i)
@@ -135,10 +132,10 @@
         block = kv.at[kind, at(plane, origin(zi), yy)]
         remote(block, block, z_send.at[0, 0], y_recv.at[zi, i, way], (ctx, (tp + 1) % 8)).wait_recv()
 
-    def x_copy(zi, i):
+    def x_copy(zi, far):
         block = kv.at[1, at(x, origin(zi), y)]
-        to = (at(x + 1 if i == 2 else 3, z, y), tp)
-        return remote(block, block, x_send.at[zi, i - 2], x_recv.at[zi, i - 2], to)
+        to = (at(x + 1 + far, z, y), tp)
+        return remote(block, block, x_send.at[zi, far], x_recv.at[zi, far], to)
 
     def x_wait(zi, i):
         kind, plane = item(i)
@@ -148,11 +145,11 @@
 
     def row_copy(kind, zi, far):
         rows = kv.at[kind, pl.ds(at(x, origin(zi), 0), 4)]
-        to = (at(3 if far else x + 1, z, y), tp)
+        to = (at(x + 1 + far, z, y), tp)
         return remote(rows, rows, r_send.at[kind, zi, far], r_recv.at[kind, zi, far], to)
 
     def row_wait(kind, zi, far):
-        rows = kv.at[kind, pl.ds(at(1 if far else x - 1, origin(zi), 0), 4)]
+        rows = kv.at[kind, pl.ds(at(x - 1 - far, origin(zi), 0), 4)]
         aside = (ctx, (tp + 1) % 8)
         remote(rows, rows, z_send.at[0, 0], r_recv.at[kind, zi, far], aside).wait_recv()
 
@@ -196,15 +193,9 @@
             z_wait(kind, zi)
         if zi in (1, 2):
             z_onward(kind, zi - 1).start()
-        if kind == 1 and zi != 1:
-
-            @pl.when(x < 3)
-            def _():
-                x_copy(zi, 2).start()
-
-            @pl.when(x == 1)
-            def _():
-                x_copy(zi, 3).start()
+        if kind == 1:
+            for far in range(2):
+                pl.when(senders(far) & ~rows_over(1, zi, x + 1 + far, far))(x_copy(zi, far).start)
 
         for way in range(3):
             y_copy(zi, kind, way).start()
@@ -215,23 +206,14 @@
 
     def rows_out(kind, zi):
         row_there(kind, zi)
-
-        @pl.when(x < 3)
-        def _():
-            row_copy(kind, zi, 0).start()
-
-        @pl.when(x == 1)
-        def _():
-            row_copy(kind, zi, 1).start()
-
-    def items():
-        return (2, x > 0), (3, x == 3)
+        for far in range(2):
+            pl.when(senders(far) & rows_over(kind, zi, x + 1 + far, far))(row_copy(kind, zi, far).start)
 
     def spread(zi):
-        for i, there in items():
-
-            @pl.when(there)
-            def _(i=i):
+        for far in range(2):
+
+            @pl.when(receivers(far) & ~rows_over(1, zi, x, far))
+            def _(i=far + 2):
                 x_wait(zi, i)
                 for way in range(3):
                     y_copy(zi, i, way).start()
@@ -245,6 +227,38 @@
         @pl.when(bundle < 15)
         def _():
             next_copy().start()
+
+    def sent(zi):
+        for i in (0, 1):
+            for way in range(3):
+                y_copy(zi, i, way).wait_send()
+        for far in range(2):
+
+            @pl.when(senders(far))
+            def _(far=far):
+                row_copy(0, zi, far).wait_send()
+                over = rows_over(1, zi, x + 1 + far, far)
+                pl.when(over)(lambda: row_copy(1, zi, far).wait_send())
+                pl.when(~over)(lambda: x_copy(zi, far).wait_send())
+
+            @pl.when(receivers(far) & ~rows_over(1, zi, x, far))
+            def _(i=far + 2):
+                for way in range(3):
+                    y_copy(zi, i, way).wait_send()
+
+    def sent_early():
+        for kind in range(2):
+            for zi in (1, 2):
+                z_copy(kind, zi).wait_send()
+                z_onward(kind, zi - 1).wait_send()
+        for d in (1, 2, 3):
+            s_copy(d).wait_send()
+        for d in range(1, 8):
+            p_copy(d).wait_send()
+        pl.when(bundle < 15)(lambda: next_copy().wait_send())
+        pl.when(x >= 2)(lambda: q_copy().wait_send())
+        for zi in (0, 1, 2):
+            sent(zi)
 
     def attend(slot, keys, values, hide):
         s = lax.dot_general(keys, qs[slot], NT, preferred_element_type=F32)
@@ -279,6 +293,11 @@
 
         keys, values = [jnp.concatenate([row(k, *r) for r in rows], axis=0) for k in (0, 1)]
         attend(slot, keys, values, hide)
+
+    def out_copy(which, h):
+        c = pl.ds(h * HEAD, HEAD)
+        out = (self_out, cross_out)[which]
+        return pltpu.make_async_copy(result.at[which, :, c], out.at[:, c], out_sem.at[which, h])
 
     def attend_panels():
         reset(3)
@@ -310,13 +329,19 @@
         factor = jnp.tanh(jnp.full((1, COLS), gate[0], F32)) / jnp.sum(tot[3], axis=0, keepdims=True)
         for h in range(GROUP):
             c = slice(h * TOK, (h + 1) * TOK)
-            cross_out[:, h * HEAD : (h + 1) * HEAD] = (acc[3, :, c] * factor[:, c]).T.astype(BF16)
+            result[1, :, c] = (acc[3, :, c] * factor[:, c]).T.astype(BF16)
+            out_copy(1, h).start()
 
     for kind in range(2):
         for zi in (1, 2):
             z_copy(kind, zi).start()
     for kind in range(2):
         block_out(kind, 0)
+    own_panel.wait()
+    pair = jnp.concatenate([panel_in[0, 0].astype(F32), panel_in[1, 0].astype(F32)], axis=0)
+    for h in range(GROUP):
+        staged[h] = pair[:, h * HEAD : (h + 1) * HEAD].astype(BF16)
+
     for d in range(1, 8):
         p_copy(d).start()
     wait_queries(0, 3)
@@ -324,6 +349,13 @@
     @pl.when(x >= 2)
     def _():
         q_copy().start()
+
+    reset(0)
+
+    @pl.when(x == 0)
+    def _():
+        reset(1)
+        reset(2)
 
     pan[y, tp] = staged[tp]
     rows_out(0, 0)
@@ -336,25 +368,29 @@
             for zi in (1, 2):
                 block_out(0, zi)
 
-            panels_out()
             for zi in (1, 2):
                 block_out(1, zi)
+            panels_out()
             rows_out(0, 1)
             block_out(0, 3)
             rows_out(0, 2)
+            spread(1)
             spread(2)
 
         @pl.when(t == 2)
         def _():
             block_out(1, 3)
             rows_out(1, 1)
+            rows_out(1, 2)
 
         @pl.when(t == 3)
         def _():
             rows_out(0, 3)
             spread(3)
 
-        @pl.when(t == jnp.where(x == 0, 6, 3))
+        pl.when(t == jnp.where(x == 0, 8, 6))(sent_early)
+
+        @pl.when(t == jnp.where(x == 0, 7, 3))
         def _():
             attend_panels()
 
@@ -369,17 +405,18 @@
     def first_use(zi, j):
         @pl.when(j == 0)
         def _():
-            if zi > 1:
-                row_there(1, zi)
-
-        for k, there in ((1, x > 0), (2, x == 3)):
-
-            @pl.when((j == k) & there)
+            if zi == 3:
+                row_there(1, 3)
+
+        for k in range(1, 3):
+
+            @pl.when((j == k) & receivers(k - 1))
             def _(k=k):
                 row_wait(0, zi, k - 1)
-                if zi == 1:
-                    row_wait(1, zi, k - 1)
-                else:
+                pl.when(rows_over(1, zi, x, k - 1))(lambda: row_wait(1, zi, k - 1))
+
+                @pl.when(~rows_over(1, zi, x, k - 1))
+                def _():
                     for way in range(3):
                         y_wait(zi, k + 1, way)
 
@@ -391,14 +428,14 @@
         def _():
             q_wait(2)
 
-        @pl.when((x == 0) & (t == 4))
+        @pl.when((x == 0) & (t == 3))
         def _():
             q_wait(1)
 
         slot = jnp.where(x == 0, j, 0)
         plane = jnp.where(x == 0, 0, x - j)
         both = (step == 3) & (x == 3)
-        fresh = (step > 0) & ((x > 0) | (t < 4))
+        fresh = (step > 0) & ((x > 0) | (t == 2) | (t == 5))
         wait_j = jnp.where(x == 0, 0, j)
         for k in range(4):
             hit = (zi == k) if k in (0, 3) else (zi == k) | (step == 2)
@@ -408,9 +445,9 @@
                 first_use(k, wait_j)
                 pl.when(both)(lambda: first_use(k, 2))
 
-        single, below, above, far = origin(zi), origin(1), origin(2), origin(3)
-
-        @pl.when(((step == 1) & ((j > 0) | (single <= z))) | ((step == 3) & (x < 3)))
+        single, below, above = origin(zi), origin(1), origin(2)
+
+        @pl.when(((step == 1) & ((j > 0) | (single <= z))) | ((step == 3) & ~both))
         def _():
             attend_rows(slot, ((plane, single),), True)
 
@@ -418,13 +455,13 @@
         def _():
             attend_rows(slot, ((plane, below), (plane, above)), True)
 
-        @pl.when(((step == 2) & (j > 0)) | both | (step == 4))
-        def _():
-            one = jnp.where(step == 2, below, jnp.where(step == 3, single, z))
-            two = jnp.where(step == 2, above, jnp.where(step == 3, single, far))
+        @pl.when(((step == 2) & (j > 0)) | both)
+        def _():
+            one = jnp.where(step == 2, below, single)
+            two = jnp.where(step == 2, above, single)
             attend_rows(slot, ((plane, one), (jnp.where(step == 3, plane - 1, plane), two)), False)
 
-        for when, slot_out in ((3, 2), (5, 1)):
+        for when, slot_out in ((5, 2), (6, 1)):
 
             @pl.when((x == 0) & (t == when))
             def _(slot_out=slot_out):
@@ -435,12 +472,12 @@
     def digits(values):
         return sum(v * 8**k for k, v in enumerate(values))
 
-    first = "11212421", "00131013", "02221100"
-    others = "13231330", "00123130", "01010110"
+    first = "112211121", "001103313", "022112100"
+    others = "132313300", "001231300", "010101100"
     plan = tuple(
         jnp.where(x == 0, digits(map(int, a)), digits(map(int, b))) for a, b in zip(first, others)
     )
-    lax.fori_loop(0, 8, turn, plan)
+    lax.fori_loop(0, 9, turn, plan)
 
     @pl.when(x >= 2)
     def _():
@@ -458,52 +495,10 @@
     inverse = 1.0 / jnp.sum(tot[0], axis=0, keepdims=True)
     for h in range(GROUP):
         c = slice(h * TOK, (h + 1) * TOK)
-        self_out[:, h * HEAD : (h + 1) * HEAD] = (acc[0, :, c] * inverse[:, c]).T.astype(BF16)
-
-    for kind in range(2):
-        for zi in (1, 2):
-            z_copy(kind, zi).wait_send()
-            z_onward(kind, zi - 1).wait_send()
-    for d in (1, 2, 3):
-        s_copy(d).wait_send()
-    for d in range(1, 8):
-        p_copy(d).wait_send()
-
-    @pl.when(bundle < 15)
-    def _():
-        next_copy().wait_send()
-
-    for zi in range(4):
-        for i in (0, 1):
-            for way in range(3):
-                y_copy(zi, i, way).wait_send()
-        if zi != 1:
-            for i, there in items():
-
-                @pl.when(there)
-                def _(i=i, zi=zi):
-                    for way in range(3):
-                        y_copy(zi, i, way).wait_send()
-
-        @pl.when(x < 3)
-        def _(zi=zi):
-            row_copy(0, zi, 0).wait_send()
-            if zi == 1:
-                row_copy(1, zi, 0).wait_send()
-            else:
-                x_copy(zi, 2).wait_send()
-
-        @pl.when(x == 1)
-        def _(zi=zi):
-            row_copy(0, zi, 1).wait_send()
-            if zi == 1:
-                row_copy(1, zi, 1).wait_send()
-            else:
-                x_copy(zi, 3).wait_send()
-
-    @pl.when(x >= 2)
-    def _():
-        q_copy().wait_send()
+        result[0, :, c] = (acc[0, :, c] * inverse[:, c]).T.astype(BF16)
+        out_copy(0, h).start()
+
+    sent(3)
 
     @pl.when(x == 0)
     def _():
@@ -511,10 +506,13 @@
             for copy in o_copies(slot):
                 copy.wait_send()
 
+    for which in range(2):
+        for h in range(GROUP):
+            out_copy(which, h).wait()
+
 
 def local(query_self, key_value_self, query_cross, panels, image_span, panel_image, cross_gate):
     smem = pl.BlockSpec(memory_space=pltpu.SMEM)
-    vmem = pl.BlockSpec(memory_space=pltpu.VMEM)
     hbm = pl.BlockSpec(memory_space=pltpu.HBM)
     dma = pltpu.SemaphoreType.DMA
     shape = jax.ShapeDtypeStruct((TOK, COLS), BF16)
@@ -522,7 +520,7 @@
         kernel,
         out_shape=(shape, shape),
         in_specs=[smem] * 3 + [hbm] * 4,
-        out_specs=(vmem, vmem),
+        out_specs=(hbm, hbm),
         scratch_shapes=[
             pltpu.VMEM((4, COLS, HEAD), BF16),
             pltpu.VMEM((2, 64, TOK, HEAD), BF16),
@@ -536,14 +534,15 @@
             pltpu.VMEM((2, 8, COLS), F32),
             pltpu.VMEM((8, COLS), F32),
             dma((4, 2)), dma((4, 2)),
-            dma((4, 2)), dma((4, 2)),
-            dma((4, 4, 3)), dma((4, 4, 3)),
-            dma((2, 4, 2)), dma((2, 4, 2)),
+            dma((4, 3)), dma((4, 3)),
+            dma((4, 5, 3)), dma((4, 5, 3)),
+            dma((2, 4, 3)), dma((2, 4, 3)),
             dma, dma((3,)),
             dma((2, 2)), dma((2,)),
             dma((8,)), dma((8,)),
             dma((4,)), dma((8,)),
             pltpu.VMEM((2, 1, 8, COLS), BF16), dma((5,)),
+            pltpu.VMEM((2, TOK, COLS), BF16), dma((2, GROUP)),
         ],
         compiler_params=pltpu.CompilerParams(
             collective_id=0, has_side_effects=True, vmem_limit_bytes=64 << 20

time: 54.4 us -> 54.2 us (level)
  the two profiles are of different devices: /device:TPU:4 before, /device:TPU:6 now
where the time goes in v4:
time: 54.2 us; the launch traced here: 54 us
  Pallas kernels  50.2 us (93%)
  local copies, waits for them, and re-layouts  2.42 us (4%)
  between operations  1.3 us (2%)
    pallas_call x1, Pallas kernels, local(): pl.pallas_call(kernel, out_shape=(shape, shape), in_specs=[smem] * 3 + [h...  50.2 us
    unnamed x4, local copies, waits for them, and re-layouts  2.42 us

profile of v4, /device:TPU:6, one launch (start us, length us, event | category | flops | bytes accessed | tf_op | source)
XLA Modules:
  0.0 54.0 jit_solution(2101793433967438030)
XLA Ops:
  1.3 50.2 %attention.1 = (bf16[128,1024]{1,0:T(8,128)(2,1)}, bf16[128,1024]{1,0:T(8,128)(2,1)}) custom-call(s32[2,64]{1,0:T(2,128)} %bitcast.1, s32[64]{0:T(128)} %slot_image.1, f32[1]{0:T(128)S(6)} %copy.11.gate, bf16[128,1024]{1,0:T(8,128)(2,1)} %q_self.1, bf16[2,128,128]{2,1,0:T(8,128)(2,1)} %kv_own.1, bf16[128,1024]{1,0:T(8,128)(2,1)} %q_cross.1, ...), custom_call_target="tpu_custom_call" | custom-call | tf_op jit(solution)/shard_map/attention/pallas_call | solution.py:519
  51.5 0.0 copy-start
  51.5 1.7 %copy.12 = bf16[128,1024]{1,0:T(8,128)(2,1)} copy(bf16[128,1024]{1,0:T(8,128)(2,1)} %get-tuple-element.4) | data formatting | bytes 524288
  53.2 0.0 copy-done
  53.2 0.7 %copy.13 = bf16[128,1024]{1,0:T(8,128)(2,1)} copy(bf16[128,1024]{1,0:T(8,128)(2,1)S(1)} %copy-done) | data formatting | bytes 524288
Async XLA Ops:
  51.5 1.7 %copy-start = (bf16[128,1024]{1,0:T(8,128)(2,1)S(1)}, bf16[128,1024]{1,0:T(8,128)(2,1)}, u32[]{:S(2)}) copy-start(bf16[128,1024]{1,0:T(8,128)(2,1)} %get-tuple-element.5) | copy-start | bytes 786436
